TPU v7x, 512 devices: a whole 4x4x16 slice. The times are simulated.
512 devices in a mesh: dp: 32 (over x, z_hi, core), tensor: 16 (over z_lo, y).
Axes of the slice: x: 4, y: 4, z: 16 (z_hi: 4, z_lo: 4; z = z_hi * 4 + z_lo), core: 2. Of those that a mesh axis runs over, the one named last changes fastest.
Arguments:
- activations: bfloat16 [2, 32768, 4096], P(None, 'dp', 'tensor'), may hold values from -6 to 6
- out_grads: bfloat16 [2, 32768, 4096], P(None, 'dp', 'tensor'), may hold values from -6 to 6
- proj_in: bfloat16 [2, 64, 4096], P(None, None, 'tensor'), may hold values from -0.09375 to 0.09375
- proj_out: bfloat16 [2, 64, 4096], P(None, None, 'tensor'), may hold values from -0.09375 to 0.09375
- example_ids: int32 [32, 1024], P('dp'), may hold values from 0 to 15, never falling along the last dimension, each value on 1 to 128 neighbouring positions
- loss_mask: int32 [32, 1024], P('dp'), may hold values 0 or 1
- query_grads: bfloat16 [69632, 2, 4096], P(('dp', 'tensor')), may hold values from -0.009765625 to 0.009765625
Outputs:
- scores: float32 [69632, 512], P(('dp', 'tensor'))
Inputs may be any that keep to these rules, and one draw needn't show every extreme that they name: `example_ids`: along each row ids never fall; each of the 16 examples of a row has 1 to 128 tokens, and one has exactly 128.
All inputs are finite; a program needn't handle non-finite values. No bound on the sum of `loss_mask` on one device may be relied on, other than what follows from the above.
Results may differ from a plain program's by a relative error of at most 0.005.
Values may be sent and summed in bfloat16 or wider, within the bound.
A program may use at most 64 MiB of HBM per device.

v0:
```python
import jax
import jax.numpy as jnp
from jax import lax
from jax.sharding import PartitionSpec as P


def from_behind(block, axis, distance):
    devices = range(lax.axis_size(axis))
    route = [((i - distance) % len(devices), i) for i in devices]
    return lax.ppermute(block, axis, route)


def spread_blocks(joined_low, local_ids, block_count, rank_width):
    grad_low = joined_low[:, :, :rank_width]
    act_low = joined_low[:, :, rank_width:]
    layers = joined_low.shape[0]
    row_count = joined_low.shape[1]
    onehot = (local_ids[:, None] == jnp.arange(block_count, dtype=jnp.int32)[None, :]).astype(
        jnp.bfloat16
    )
    spread = (onehot[None, :, :, None] * grad_low[:, :, None, :]).reshape(
        layers, row_count, block_count * rank_width
    )
    return jnp.einsum("ltj,ltk->ljk", act_low, spread, preferred_element_type=jnp.float32)


def arrange(outer_sum, block_count, rank_width):
    layers = outer_sum.shape[0]
    shaped = outer_sum.reshape(layers, rank_width, block_count, rank_width)
    return jnp.transpose(shaped, (2, 0, 3, 1)).reshape(
        block_count, layers * rank_width * rank_width
    )


def local(activations, out_grads, proj_in, proj_out, example_ids, loss_mask, query_grads):
    tok_count = activations.shape[1]
    rank_width = proj_in.shape[1]
    block_count = tok_count // 64
    token_mask = loss_mask[0].astype(jnp.float32)
    local_ids = example_ids[0]
    act_part = jnp.einsum("ltd,lrd->ltr", activations, proj_in, preferred_element_type=jnp.float32)
    grad_part = jnp.einsum("ltd,lrd->ltr", out_grads, proj_out, preferred_element_type=jnp.float32)
    joined = jnp.concatenate([grad_part * token_mask[None, :, None], act_part], axis=2)
    summed = lax.psum(joined, "tensor")
    outer_sum = spread_blocks(summed.astype(jnp.bfloat16), local_ids, block_count, rank_width)
    train_tile = arrange(outer_sum, block_count, rank_width).astype(jnp.bfloat16)
    queries = query_grads.reshape(query_grads.shape[0], -1)
    cycle_size = lax.axis_size("dp")
    own_index = lax.axis_index("dp")
    zero_index = jnp.zeros((), jnp.int32)

    def score_tile(incoming):
        return lax.dot_general(
            queries, incoming, (((1,), (1,)), ((), ())), preferred_element_type=jnp.float32
        )

    initial = jnp.zeros((queries.shape[0], block_count * cycle_size), jnp.float32)
    running = lax.dynamic_update_slice(
        initial, score_tile(train_tile), (zero_index, own_index * block_count)
    )

    def advance(turn_index, carried):
        running_scores, current = carried
        current = from_behind(current, "dp", 1)
        source = (own_index - turn_index + cycle_size) % cycle_size
        running_scores = lax.dynamic_update_slice(
            running_scores, score_tile(current), (zero_index, source * block_count)
        )
        return (running_scores, current)

    scores, latest = lax.fori_loop(1, cycle_size, advance, (running, train_tile))
    return scores


def solution(mesh):
    in_specs = (
        P(None, "dp", "tensor"),
        P(None, "dp", "tensor"),
        P(None, None, "tensor"),
        P(None, None, "tensor"),
        P("dp", None),
        P("dp", None),
        P(("dp", "tensor"), None, None),
    )
    out_specs = P(("dp", "tensor"), None)
    return jax.shard_map(local, mesh=mesh, in_specs=in_specs, out_specs=out_specs, check_vma=False)
```

profile of v0, /device:TPU:45, one launch (start us, length us, event | category | flops | bytes accessed | tf_op | source)
XLA Modules:
  0.0 675.9 jit_solution(17273172101777853191)
XLA Ops:
  3.9 67.8 %all-reduce.1 = bf16[2,1024,128]{1,2,0:T(8,128)(2,1)S(1)} all-reduce(f32[2,1024,128]{1,2,0:T(8,128)S(1)} %pad_maximum_fusion), channel_id=1, replica_groups=mesh['dp'=32,'tensor'=16] {'tensor'}, use_global_device_ids=true, to_apply=%region_0.0 | all-reduce | flops 262144 | bytes 1572864 | tf_op jit(solution)/shard_map/psum | solution.py:44
  81.9 592.1 %while.17 = (s32[]{:T(128)}, f32[136,512]{0,1:T(8,128)}, bf16[16,8192]{1,0:T(8,128)(2,1)}, bf16[136,8192]{1,0:T(8,128)(2,1)S(1)}, s32[]{:T(128)}, /*index=5*/s32...) while((s32[]{:T(128)}, f32[136,512]{0,1:T(8,128)}, ...), condition=%wide.region_2.3_spmd, body=%wide.region_1.2_spmd.sunk | while | flops 35651600 | bytes 4079948 | solution.py:71
  81.9 22.4 %collective-permute-start = (bf16[16,8192]{1,0:T(8,128)(2,1)}, bf16[16,8192]{1,0:T(8,128)(2,1)S(1)}, u32[]{:S(2)}, u32[]{:S(2)}) collective-permute-start(bf16[16,8192]{1,0:T(8,128)(2,1)} %get-tuple-element.193), channel_id=1, source_target_pairs={{496,0},{0,16},{16,32},{32,48},{48,64},{64,80},{80,96},{96,112},{1... | collective-permute-start | bytes 786440 | tf_op jit(solution)/shard_map/while/body/eval_jaxpr/ppermute | solution.py:10
  121.4 12.0 %collective-permute-done = bf16[16,8192]{1,0:T(8,128)(2,1)S(1)} collective-permute-done((bf16[16,8192]{1,0:T(8,128)(2,1)}, bf16[16,8192]{1,0:T(8,128)(2,1)S(1)}, u32[]{:S(2)}, u32[]{:S(2)}) %collective-permute-start) | collective-permute-done | bytes 262176 | tf_op jit(solution)/shard_map/while/body/eval_jaxpr/ppermute | solution.py:10
  194.1 8.4 %collective-permute-done = bf16[16,8192]{1,0:T(8,128)(2,1)S(1)} collective-permute-done((bf16[16,8192]{1,0:T(8,128)(2,1)}, bf16[16,8192]{1,0:T(8,128)(2,1)S(1)}, u32[]{:S(2)}, u32[]{:S(2)}) %collective-permute-start) | collective-permute-done | bytes 262176 | tf_op jit(solution)/shard_map/while/body/eval_jaxpr/ppermute | solution.py:10
  204.6 8.3 %collective-permute-start = (bf16[16,8192]{1,0:T(8,128)(2,1)}, bf16[16,8192]{1,0:T(8,128)(2,1)S(1)}, u32[]{:S(2)}, u32[]{:S(2)}) collective-permute-start(bf16[16,8192]{1,0:T(8,128)(2,1)} %get-tuple-element.193), channel_id=1, source_target_pairs={{496,0},{0,16},{16,32},{32,48},{48,64},{64,80},{80,96},{96,112},{1... | collective-permute-start | bytes 786440 | tf_op jit(solution)/shard_map/while/body/eval_jaxpr/ppermute | solution.py:10
  212.9 11.9 %collective-permute-done = bf16[16,8192]{1,0:T(8,128)(2,1)S(1)} collective-permute-done((bf16[16,8192]{1,0:T(8,128)(2,1)}, bf16[16,8192]{1,0:T(8,128)(2,1)S(1)}, u32[]{:S(2)}, u32[]{:S(2)}) %collective-permute-start) | collective-permute-done | bytes 262176 | tf_op jit(solution)/shard_map/while/body/eval_jaxpr/ppermute | solution.py:10
  226.8 8.4 %collective-permute-start = (bf16[16,8192]{1,0:T(8,128)(2,1)}, bf16[16,8192]{1,0:T(8,128)(2,1)S(1)}, u32[]{:S(2)}, u32[]{:S(2)}) collective-permute-start(bf16[16,8192]{1,0:T(8,128)(2,1)} %get-tuple-element.193), channel_id=1, source_target_pairs={{496,0},{0,16},{16,32},{32,48},{48,64},{64,80},{80,96},{96,112},{1... | collective-permute-start | bytes 786440 | tf_op jit(solution)/shard_map/while/body/eval_jaxpr/ppermute | solution.py:10
  293.9 8.3 %collective-permute-start = (bf16[16,8192]{1,0:T(8,128)(2,1)}, bf16[16,8192]{1,0:T(8,128)(2,1)S(1)}, u32[]{:S(2)}, u32[]{:S(2)}) collective-permute-start(bf16[16,8192]{1,0:T(8,128)(2,1)} %get-tuple-element.193), channel_id=1, source_target_pairs={{496,0},{0,16},{16,32},{32,48},{48,64},{64,80},{80,96},{96,112},{1... | collective-permute-start | bytes 786440 | tf_op jit(solution)/shard_map/while/body/eval_jaxpr/ppermute | solution.py:10
  302.3 9.1 %collective-permute-done = bf16[16,8192]{1,0:T(8,128)(2,1)S(1)} collective-permute-done((bf16[16,8192]{1,0:T(8,128)(2,1)}, bf16[16,8192]{1,0:T(8,128)(2,1)S(1)}, u32[]{:S(2)}, u32[]{:S(2)}) %collective-permute-start) | collective-permute-done | bytes 262176 | tf_op jit(solution)/shard_map/while/body/eval_jaxpr/ppermute | solution.py:10
  340.1 9.4 %collective-permute-done = bf16[16,8192]{1,0:T(8,128)(2,1)S(1)} collective-permute-done((bf16[16,8192]{1,0:T(8,128)(2,1)}, bf16[16,8192]{1,0:T(8,128)(2,1)S(1)}, u32[]{:S(2)}, u32[]{:S(2)}) %collective-permute-start) | collective-permute-done | bytes 262176 | tf_op jit(solution)/shard_map/while/body/eval_jaxpr/ppermute | solution.py:10
  351.5 8.3 %collective-permute-start = (bf16[16,8192]{1,0:T(8,128)(2,1)}, bf16[16,8192]{1,0:T(8,128)(2,1)S(1)}, u32[]{:S(2)}, u32[]{:S(2)}) collective-permute-start(bf16[16,8192]{1,0:T(8,128)(2,1)} %get-tuple-element.193), channel_id=1, source_target_pairs={{496,0},{0,16},{16,32},{32,48},{48,64},{64,80},{80,96},{96,112},{1... | collective-permute-start | bytes 786440 | tf_op jit(solution)/shard_map/while/body/eval_jaxpr/ppermute | solution.py:10
  359.8 9.0 %collective-permute-done = bf16[16,8192]{1,0:T(8,128)(2,1)S(1)} collective-permute-done((bf16[16,8192]{1,0:T(8,128)(2,1)}, bf16[16,8192]{1,0:T(8,128)(2,1)S(1)}, u32[]{:S(2)}, u32[]{:S(2)}) %collective-permute-start) | collective-permute-done | bytes 262176 | tf_op jit(solution)/shard_map/while/body/eval_jaxpr/ppermute | solution.py:10
  389.3 8.3 %collective-permute-start = (bf16[16,8192]{1,0:T(8,128)(2,1)}, bf16[16,8192]{1,0:T(8,128)(2,1)S(1)}, u32[]{:S(2)}, u32[]{:S(2)}) collective-permute-start(bf16[16,8192]{1,0:T(8,128)(2,1)} %get-tuple-element.193), channel_id=1, source_target_pairs={{496,0},{0,16},{16,32},{32,48},{48,64},{64,80},{80,96},{96,112},{1... | collective-permute-start | bytes 786440 | tf_op jit(solution)/shard_map/while/body/eval_jaxpr/ppermute | solution.py:10
  397.6 9.4 %collective-permute-done = bf16[16,8192]{1,0:T(8,128)(2,1)S(1)} collective-permute-done((bf16[16,8192]{1,0:T(8,128)(2,1)}, bf16[16,8192]{1,0:T(8,128)(2,1)S(1)}, u32[]{:S(2)}, u32[]{:S(2)}) %collective-permute-start) | collective-permute-done | bytes 262176 | tf_op jit(solution)/shard_map/while/body/eval_jaxpr/ppermute | solution.py:10
  409.0 8.3 %collective-permute-start = (bf16[16,8192]{1,0:T(8,128)(2,1)}, bf16[16,8192]{1,0:T(8,128)(2,1)S(1)}, u32[]{:S(2)}, u32[]{:S(2)}) collective-permute-start(bf16[16,8192]{1,0:T(8,128)(2,1)} %get-tuple-element.193), channel_id=1, source_target_pairs={{496,0},{0,16},{16,32},{32,48},{48,64},{64,80},{80,96},{96,112},{1... | collective-permute-start | bytes 786440 | tf_op jit(solution)/shard_map/while/body/eval_jaxpr/ppermute | solution.py:10
  417.4 9.0 %collective-permute-done = bf16[16,8192]{1,0:T(8,128)(2,1)S(1)} collective-permute-done((bf16[16,8192]{1,0:T(8,128)(2,1)}, bf16[16,8192]{1,0:T(8,128)(2,1)S(1)}, u32[]{:S(2)}, u32[]{:S(2)}) %collective-permute-start) | collective-permute-done | bytes 262176 | tf_op jit(solution)/shard_map/while/body/eval_jaxpr/ppermute | solution.py:10
  446.8 8.3 %collective-permute-start = (bf16[16,8192]{1,0:T(8,128)(2,1)}, bf16[16,8192]{1,0:T(8,128)(2,1)S(1)}, u32[]{:S(2)}, u32[]{:S(2)}) collective-permute-start(bf16[16,8192]{1,0:T(8,128)(2,1)} %get-tuple-element.193), channel_id=1, source_target_pairs={{496,0},{0,16},{16,32},{32,48},{48,64},{64,80},{80,96},{96,112},{1... | collective-permute-start | bytes 786440 | tf_op jit(solution)/shard_map/while/body/eval_jaxpr/ppermute | solution.py:10
  455.1 9.4 %collective-permute-done = bf16[16,8192]{1,0:T(8,128)(2,1)S(1)} collective-permute-done((bf16[16,8192]{1,0:T(8,128)(2,1)}, bf16[16,8192]{1,0:T(8,128)(2,1)S(1)}, u32[]{:S(2)}, u32[]{:S(2)}) %collective-permute-start) | collective-permute-done | bytes 262176 | tf_op jit(solution)/shard_map/while/body/eval_jaxpr/ppermute | solution.py:10
  466.6 8.4 %collective-permute-start = (bf16[16,8192]{1,0:T(8,128)(2,1)}, bf16[16,8192]{1,0:T(8,128)(2,1)S(1)}, u32[]{:S(2)}, u32[]{:S(2)}) collective-permute-start(bf16[16,8192]{1,0:T(8,128)(2,1)} %get-tuple-element.193), channel_id=1, source_target_pairs={{496,0},{0,16},{16,32},{32,48},{48,64},{64,80},{80,96},{96,112},{1... | collective-permute-start | bytes 786440 | tf_op jit(solution)/shard_map/while/body/eval_jaxpr/ppermute | solution.py:10
  475.0 9.0 %collective-permute-done = bf16[16,8192]{1,0:T(8,128)(2,1)S(1)} collective-permute-done((bf16[16,8192]{1,0:T(8,128)(2,1)}, bf16[16,8192]{1,0:T(8,128)(2,1)S(1)}, u32[]{:S(2)}, u32[]{:S(2)}) %collective-permute-start) | collective-permute-done | bytes 262176 | tf_op jit(solution)/shard_map/while/body/eval_jaxpr/ppermute | solution.py:10
  504.3 8.3 %collective-permute-start = (bf16[16,8192]{1,0:T(8,128)(2,1)}, bf16[16,8192]{1,0:T(8,128)(2,1)S(1)}, u32[]{:S(2)}, u32[]{:S(2)}) collective-permute-start(bf16[16,8192]{1,0:T(8,128)(2,1)} %get-tuple-element.193), channel_id=1, source_target_pairs={{496,0},{0,16},{16,32},{32,48},{48,64},{64,80},{80,96},{96,112},{1... | collective-permute-start | bytes 786440 | tf_op jit(solution)/shard_map/while/body/eval_jaxpr/ppermute | solution.py:10
  512.7 9.5 %collective-permute-done = bf16[16,8192]{1,0:T(8,128)(2,1)S(1)} collective-permute-done((bf16[16,8192]{1,0:T(8,128)(2,1)}, bf16[16,8192]{1,0:T(8,128)(2,1)S(1)}, u32[]{:S(2)}, u32[]{:S(2)}) %collective-permute-start) | collective-permute-done | bytes 262176 | tf_op jit(solution)/shard_map/while/body/eval_jaxpr/ppermute | solution.py:10
  524.2 8.4 %collective-permute-start = (bf16[16,8192]{1,0:T(8,128)(2,1)}, bf16[16,8192]{1,0:T(8,128)(2,1)S(1)}, u32[]{:S(2)}, u32[]{:S(2)}) collective-permute-start(bf16[16,8192]{1,0:T(8,128)(2,1)} %get-tuple-element.193), channel_id=1, source_target_pairs={{496,0},{0,16},{16,32},{32,48},{48,64},{64,80},{80,96},{96,112},{1... | collective-permute-start | bytes 786440 | tf_op jit(solution)/shard_map/while/body/eval_jaxpr/ppermute | solution.py:10
  532.6 8.9 %collective-permute-done = bf16[16,8192]{1,0:T(8,128)(2,1)S(1)} collective-permute-done((bf16[16,8192]{1,0:T(8,128)(2,1)}, bf16[16,8192]{1,0:T(8,128)(2,1)S(1)}, u32[]{:S(2)}, u32[]{:S(2)}) %collective-permute-start) | collective-permute-done | bytes 262176 | tf_op jit(solution)/shard_map/while/body/eval_jaxpr/ppermute | solution.py:10
  561.8 8.3 %collective-permute-start = (bf16[16,8192]{1,0:T(8,128)(2,1)}, bf16[16,8192]{1,0:T(8,128)(2,1)S(1)}, u32[]{:S(2)}, u32[]{:S(2)}) collective-permute-start(bf16[16,8192]{1,0:T(8,128)(2,1)} %get-tuple-element.193), channel_id=1, source_target_pairs={{496,0},{0,16},{16,32},{32,48},{48,64},{64,80},{80,96},{96,112},{1... | collective-permute-start | bytes 786440 | tf_op jit(solution)/shard_map/while/body/eval_jaxpr/ppermute | solution.py:10
  570.2 9.6 %collective-permute-done = bf16[16,8192]{1,0:T(8,128)(2,1)S(1)} collective-permute-done((bf16[16,8192]{1,0:T(8,128)(2,1)}, bf16[16,8192]{1,0:T(8,128)(2,1)S(1)}, u32[]{:S(2)}, u32[]{:S(2)}) %collective-permute-start) | collective-permute-done | bytes 262176 | tf_op jit(solution)/shard_map/while/body/eval_jaxpr/ppermute | solution.py:10
  581.7 8.4 %collective-permute-start = (bf16[16,8192]{1,0:T(8,128)(2,1)}, bf16[16,8192]{1,0:T(8,128)(2,1)S(1)}, u32[]{:S(2)}, u32[]{:S(2)}) collective-permute-start(bf16[16,8192]{1,0:T(8,128)(2,1)} %get-tuple-element.193), channel_id=1, source_target_pairs={{496,0},{0,16},{16,32},{32,48},{48,64},{64,80},{80,96},{96,112},{1... | collective-permute-start | bytes 786440 | tf_op jit(solution)/shard_map/while/body/eval_jaxpr/ppermute | solution.py:10
  590.1 8.8 %collective-permute-done = bf16[16,8192]{1,0:T(8,128)(2,1)S(1)} collective-permute-done((bf16[16,8192]{1,0:T(8,128)(2,1)}, bf16[16,8192]{1,0:T(8,128)(2,1)S(1)}, u32[]{:S(2)}, u32[]{:S(2)}) %collective-permute-start) | collective-permute-done | bytes 262176 | tf_op jit(solution)/shard_map/while/body/eval_jaxpr/ppermute | solution.py:10
  627.7 9.6 %collective-permute-done = bf16[16,8192]{1,0:T(8,128)(2,1)S(1)} collective-permute-done((bf16[16,8192]{1,0:T(8,128)(2,1)}, bf16[16,8192]{1,0:T(8,128)(2,1)S(1)}, u32[]{:S(2)}, u32[]{:S(2)}) %collective-permute-start) | collective-permute-done | bytes 262176 | tf_op jit(solution)/shard_map/while/body/eval_jaxpr/ppermute | solution.py:10
  639.3 8.4 %collective-permute-start = (bf16[16,8192]{1,0:T(8,128)(2,1)}, bf16[16,8192]{1,0:T(8,128)(2,1)S(1)}, u32[]{:S(2)}, u32[]{:S(2)}) collective-permute-start(bf16[16,8192]{1,0:T(8,128)(2,1)} %get-tuple-element.193), channel_id=1, source_target_pairs={{496,0},{0,16},{16,32},{32,48},{48,64},{64,80},{80,96},{96,112},{1... | collective-permute-start | bytes 786440 | tf_op jit(solution)/shard_map/while/body/eval_jaxpr/ppermute | solution.py:10
  647.7 8.8 %collective-permute-done = bf16[16,8192]{1,0:T(8,128)(2,1)S(1)} collective-permute-done((bf16[16,8192]{1,0:T(8,128)(2,1)}, bf16[16,8192]{1,0:T(8,128)(2,1)S(1)}, u32[]{:S(2)}, u32[]{:S(2)}) %collective-permute-start) | collective-permute-done | bytes 262176 | tf_op jit(solution)/shard_map/while/body/eval_jaxpr/ppermute | solution.py:10
  (116 shorter events, 324.2 us)
Async XLA Ops:
  3.8 67.9 %copy-start.2 = (s32[1,1024]{1,0:T(1,128)S(1)}, s32[1,1024]{1,0:T(1,128)}, u32[]{:S(2)}) copy-start(s32[1,1024]{1,0:T(1,128)} %param.13) | copy-start | bytes 12292
  81.9 29.2 %collective-permute-start = (bf16[16,8192]{1,0:T(8,128)(2,1)}, bf16[16,8192]{1,0:T(8,128)(2,1)S(1)}, u32[]{:S(2)}, u32[]{:S(2)}) collective-permute-start(bf16[16,8192]{1,0:T(8,128)(2,1)} %get-tuple-element.193), channel_id=1, source_target_pairs={{496,0},{0,16},{16,32},{32,48},{48,64},{64,80},{80,96},{96,112},{1... | collective-permute-start | bytes 786440 | tf_op jit(solution)/shard_map/while/body/eval_jaxpr/ppermute | solution.py:10
  113.1 20.2 %collective-permute-start = (bf16[16,8192]{1,0:T(8,128)(2,1)}, bf16[16,8192]{1,0:T(8,128)(2,1)S(1)}, u32[]{:S(2)}, u32[]{:S(2)}) collective-permute-start(bf16[16,8192]{1,0:T(8,128)(2,1)} %get-tuple-element.193), channel_id=1, source_target_pairs={{496,0},{0,16},{16,32},{32,48},{48,64},{64,80},{80,96},{96,112},{1... | collective-permute-start | bytes 786440 | tf_op jit(solution)/shard_map/while/body/eval_jaxpr/ppermute | solution.py:10
  135.3 15.1 %collective-permute-start = (bf16[16,8192]{1,0:T(8,128)(2,1)}, bf16[16,8192]{1,0:T(8,128)(2,1)S(1)}, u32[]{:S(2)}, u32[]{:S(2)}) collective-permute-start(bf16[16,8192]{1,0:T(8,128)(2,1)} %get-tuple-element.193), channel_id=1, source_target_pairs={{496,0},{0,16},{16,32},{32,48},{48,64},{64,80},{80,96},{96,112},{1... | collective-permute-start | bytes 786440 | tf_op jit(solution)/shard_map/while/body/eval_jaxpr/ppermute | solution.py:10
  152.4 13.8 %collective-permute-start = (bf16[16,8192]{1,0:T(8,128)(2,1)}, bf16[16,8192]{1,0:T(8,128)(2,1)S(1)}, u32[]{:S(2)}, u32[]{:S(2)}) collective-permute-start(bf16[16,8192]{1,0:T(8,128)(2,1)} %get-tuple-element.193), channel_id=1, source_target_pairs={{496,0},{0,16},{16,32},{32,48},{48,64},{64,80},{80,96},{96,112},{1... | collective-permute-start | bytes 786440 | tf_op jit(solution)/shard_map/while/body/eval_jaxpr/ppermute | solution.py:10
  168.3 15.5 %collective-permute-start = (bf16[16,8192]{1,0:T(8,128)(2,1)}, bf16[16,8192]{1,0:T(8,128)(2,1)S(1)}, u32[]{:S(2)}, u32[]{:S(2)}) collective-permute-start(bf16[16,8192]{1,0:T(8,128)(2,1)} %get-tuple-element.193), channel_id=1, source_target_pairs={{496,0},{0,16},{16,32},{32,48},{48,64},{64,80},{80,96},{96,112},{1... | collective-permute-start | bytes 786440 | tf_op jit(solution)/shard_map/while/body/eval_jaxpr/ppermute | solution.py:10
  185.8 16.7 %collective-permute-start = (bf16[16,8192]{1,0:T(8,128)(2,1)}, bf16[16,8192]{1,0:T(8,128)(2,1)S(1)}, u32[]{:S(2)}, u32[]{:S(2)}) collective-permute-start(bf16[16,8192]{1,0:T(8,128)(2,1)} %get-tuple-element.193), channel_id=1, source_target_pairs={{496,0},{0,16},{16,32},{32,48},{48,64},{64,80},{80,96},{96,112},{1... | collective-permute-start | bytes 786440 | tf_op jit(solution)/shard_map/while/body/eval_jaxpr/ppermute | solution.py:10
  204.6 20.3 %collective-permute-start = (bf16[16,8192]{1,0:T(8,128)(2,1)}, bf16[16,8192]{1,0:T(8,128)(2,1)S(1)}, u32[]{:S(2)}, u32[]{:S(2)}) collective-permute-start(bf16[16,8192]{1,0:T(8,128)(2,1)} %get-tuple-element.193), channel_id=1, source_target_pairs={{496,0},{0,16},{16,32},{32,48},{48,64},{64,80},{80,96},{96,112},{1... | collective-permute-start | bytes 786440 | tf_op jit(solution)/shard_map/while/body/eval_jaxpr/ppermute | solution.py:10
  226.8 14.0 %collective-permute-start = (bf16[16,8192]{1,0:T(8,128)(2,1)}, bf16[16,8192]{1,0:T(8,128)(2,1)S(1)}, u32[]{:S(2)}, u32[]{:S(2)}) collective-permute-start(bf16[16,8192]{1,0:T(8,128)(2,1)} %get-tuple-element.193), channel_id=1, source_target_pairs={{496,0},{0,16},{16,32},{32,48},{48,64},{64,80},{80,96},{96,112},{1... | collective-permute-start | bytes 786440 | tf_op jit(solution)/shard_map/while/body/eval_jaxpr/ppermute | solution.py:10
  242.8 14.4 %collective-permute-start = (bf16[16,8192]{1,0:T(8,128)(2,1)}, bf16[16,8192]{1,0:T(8,128)(2,1)S(1)}, u32[]{:S(2)}, u32[]{:S(2)}) collective-permute-start(bf16[16,8192]{1,0:T(8,128)(2,1)} %get-tuple-element.193), channel_id=1, source_target_pairs={{496,0},{0,16},{16,32},{32,48},{48,64},{64,80},{80,96},{96,112},{1... | collective-permute-start | bytes 786440 | tf_op jit(solution)/shard_map/while/body/eval_jaxpr/ppermute | solution.py:10
  259.2 14.4 %collective-permute-start = (bf16[16,8192]{1,0:T(8,128)(2,1)}, bf16[16,8192]{1,0:T(8,128)(2,1)S(1)}, u32[]{:S(2)}, u32[]{:S(2)}) collective-permute-start(bf16[16,8192]{1,0:T(8,128)(2,1)} %get-tuple-element.193), channel_id=1, source_target_pairs={{496,0},{0,16},{16,32},{32,48},{48,64},{64,80},{80,96},{96,112},{1... | collective-permute-start | bytes 786440 | tf_op jit(solution)/shard_map/while/body/eval_jaxpr/ppermute | solution.py:10
  275.6 16.3 %collective-permute-start = (bf16[16,8192]{1,0:T(8,128)(2,1)}, bf16[16,8192]{1,0:T(8,128)(2,1)S(1)}, u32[]{:S(2)}, u32[]{:S(2)}) collective-permute-start(bf16[16,8192]{1,0:T(8,128)(2,1)} %get-tuple-element.193), channel_id=1, source_target_pairs={{496,0},{0,16},{16,32},{32,48},{48,64},{64,80},{80,96},{96,112},{1... | collective-permute-start | bytes 786440 | tf_op jit(solution)/shard_map/while/body/eval_jaxpr/ppermute | solution.py:10
  293.9 17.5 %collective-permute-start = (bf16[16,8192]{1,0:T(8,128)(2,1)}, bf16[16,8192]{1,0:T(8,128)(2,1)S(1)}, u32[]{:S(2)}, u32[]{:S(2)}) collective-permute-start(bf16[16,8192]{1,0:T(8,128)(2,1)} %get-tuple-element.193), channel_id=1, source_target_pairs={{496,0},{0,16},{16,32},{32,48},{48,64},{64,80},{80,96},{96,112},{1... | collective-permute-start | bytes 786440 | tf_op jit(solution)/shard_map/while/body/eval_jaxpr/ppermute | solution.py:10
  313.4 16.4 %collective-permute-start = (bf16[16,8192]{1,0:T(8,128)(2,1)}, bf16[16,8192]{1,0:T(8,128)(2,1)S(1)}, u32[]{:S(2)}, u32[]{:S(2)}) collective-permute-start(bf16[16,8192]{1,0:T(8,128)(2,1)} %get-tuple-element.193), channel_id=1, source_target_pairs={{496,0},{0,16},{16,32},{32,48},{48,64},{64,80},{80,96},{96,112},{1... | collective-permute-start | bytes 786440 | tf_op jit(solution)/shard_map/while/body/eval_jaxpr/ppermute | solution.py:10
  331.8 17.7 %collective-permute-start = (bf16[16,8192]{1,0:T(8,128)(2,1)}, bf16[16,8192]{1,0:T(8,128)(2,1)S(1)}, u32[]{:S(2)}, u32[]{:S(2)}) collective-permute-start(bf16[16,8192]{1,0:T(8,128)(2,1)} %get-tuple-element.193), channel_id=1, source_target_pairs={{496,0},{0,16},{16,32},{32,48},{48,64},{64,80},{80,96},{96,112},{1... | collective-permute-start | bytes 786440 | tf_op jit(solution)/shard_map/while/body/eval_jaxpr/ppermute | solution.py:10
  351.5 17.4 %collective-permute-start = (bf16[16,8192]{1,0:T(8,128)(2,1)}, bf16[16,8192]{1,0:T(8,128)(2,1)S(1)}, u32[]{:S(2)}, u32[]{:S(2)}) collective-permute-start(bf16[16,8192]{1,0:T(8,128)(2,1)} %get-tuple-element.193), channel_id=1, source_target_pairs={{496,0},{0,16},{16,32},{32,48},{48,64},{64,80},{80,96},{96,112},{1... | collective-permute-start | bytes 786440 | tf_op jit(solution)/shard_map/while/body/eval_jaxpr/ppermute | solution.py:10
  370.9 16.4 %collective-permute-start = (bf16[16,8192]{1,0:T(8,128)(2,1)}, bf16[16,8192]{1,0:T(8,128)(2,1)S(1)}, u32[]{:S(2)}, u32[]{:S(2)}) collective-permute-start(bf16[16,8192]{1,0:T(8,128)(2,1)} %get-tuple-element.193), channel_id=1, source_target_pairs={{496,0},{0,16},{16,32},{32,48},{48,64},{64,80},{80,96},{96,112},{1... | collective-permute-start | bytes 786440 | tf_op jit(solution)/shard_map/while/body/eval_jaxpr/ppermute | solution.py:10
  389.3 17.8 %collective-permute-start = (bf16[16,8192]{1,0:T(8,128)(2,1)}, bf16[16,8192]{1,0:T(8,128)(2,1)S(1)}, u32[]{:S(2)}, u32[]{:S(2)}) collective-permute-start(bf16[16,8192]{1,0:T(8,128)(2,1)} %get-tuple-element.193), channel_id=1, source_target_pairs={{496,0},{0,16},{16,32},{32,48},{48,64},{64,80},{80,96},{96,112},{1... | collective-permute-start | bytes 786440 | tf_op jit(solution)/shard_map/while/body/eval_jaxpr/ppermute | solution.py:10
  409.0 17.4 %collective-permute-start = (bf16[16,8192]{1,0:T(8,128)(2,1)}, bf16[16,8192]{1,0:T(8,128)(2,1)S(1)}, u32[]{:S(2)}, u32[]{:S(2)}) collective-permute-start(bf16[16,8192]{1,0:T(8,128)(2,1)} %get-tuple-element.193), channel_id=1, source_target_pairs={{496,0},{0,16},{16,32},{32,48},{48,64},{64,80},{80,96},{96,112},{1... | collective-permute-start | bytes 786440 | tf_op jit(solution)/shard_map/while/body/eval_jaxpr/ppermute | solution.py:10
  428.4 16.4 %collective-permute-start = (bf16[16,8192]{1,0:T(8,128)(2,1)}, bf16[16,8192]{1,0:T(8,128)(2,1)S(1)}, u32[]{:S(2)}, u32[]{:S(2)}) collective-permute-start(bf16[16,8192]{1,0:T(8,128)(2,1)} %get-tuple-element.193), channel_id=1, source_target_pairs={{496,0},{0,16},{16,32},{32,48},{48,64},{64,80},{80,96},{96,112},{1... | collective-permute-start | bytes 786440 | tf_op jit(solution)/shard_map/while/body/eval_jaxpr/ppermute | solution.py:10
  446.8 17.8 %collective-permute-start = (bf16[16,8192]{1,0:T(8,128)(2,1)}, bf16[16,8192]{1,0:T(8,128)(2,1)S(1)}, u32[]{:S(2)}, u32[]{:S(2)}) collective-permute-start(bf16[16,8192]{1,0:T(8,128)(2,1)} %get-tuple-element.193), channel_id=1, source_target_pairs={{496,0},{0,16},{16,32},{32,48},{48,64},{64,80},{80,96},{96,112},{1... | collective-permute-start | bytes 786440 | tf_op jit(solution)/shard_map/while/body/eval_jaxpr/ppermute | solution.py:10
  466.6 17.3 %collective-permute-start = (bf16[16,8192]{1,0:T(8,128)(2,1)}, bf16[16,8192]{1,0:T(8,128)(2,1)S(1)}, u32[]{:S(2)}, u32[]{:S(2)}) collective-permute-start(bf16[16,8192]{1,0:T(8,128)(2,1)} %get-tuple-element.193), channel_id=1, source_target_pairs={{496,0},{0,16},{16,32},{32,48},{48,64},{64,80},{80,96},{96,112},{1... | collective-permute-start | bytes 786440 | tf_op jit(solution)/shard_map/while/body/eval_jaxpr/ppermute | solution.py:10
  485.9 16.4 %collective-permute-start = (bf16[16,8192]{1,0:T(8,128)(2,1)}, bf16[16,8192]{1,0:T(8,128)(2,1)S(1)}, u32[]{:S(2)}, u32[]{:S(2)}) collective-permute-start(bf16[16,8192]{1,0:T(8,128)(2,1)} %get-tuple-element.193), channel_id=1, source_target_pairs={{496,0},{0,16},{16,32},{32,48},{48,64},{64,80},{80,96},{96,112},{1... | collective-permute-start | bytes 786440 | tf_op jit(solution)/shard_map/while/body/eval_jaxpr/ppermute | solution.py:10
  504.3 17.9 %collective-permute-start = (bf16[16,8192]{1,0:T(8,128)(2,1)}, bf16[16,8192]{1,0:T(8,128)(2,1)S(1)}, u32[]{:S(2)}, u32[]{:S(2)}) collective-permute-start(bf16[16,8192]{1,0:T(8,128)(2,1)} %get-tuple-element.193), channel_id=1, source_target_pairs={{496,0},{0,16},{16,32},{32,48},{48,64},{64,80},{80,96},{96,112},{1... | collective-permute-start | bytes 786440 | tf_op jit(solution)/shard_map/while/body/eval_jaxpr/ppermute | solution.py:10
  524.2 17.3 %collective-permute-start = (bf16[16,8192]{1,0:T(8,128)(2,1)}, bf16[16,8192]{1,0:T(8,128)(2,1)S(1)}, u32[]{:S(2)}, u32[]{:S(2)}) collective-permute-start(bf16[16,8192]{1,0:T(8,128)(2,1)} %get-tuple-element.193), channel_id=1, source_target_pairs={{496,0},{0,16},{16,32},{32,48},{48,64},{64,80},{80,96},{96,112},{1... | collective-permute-start | bytes 786440 | tf_op jit(solution)/shard_map/while/body/eval_jaxpr/ppermute | solution.py:10
  543.5 16.3 %collective-permute-start = (bf16[16,8192]{1,0:T(8,128)(2,1)}, bf16[16,8192]{1,0:T(8,128)(2,1)S(1)}, u32[]{:S(2)}, u32[]{:S(2)}) collective-permute-start(bf16[16,8192]{1,0:T(8,128)(2,1)} %get-tuple-element.193), channel_id=1, source_target_pairs={{496,0},{0,16},{16,32},{32,48},{48,64},{64,80},{80,96},{96,112},{1... | collective-permute-start | bytes 786440 | tf_op jit(solution)/shard_map/while/body/eval_jaxpr/ppermute | solution.py:10
  561.8 17.9 %collective-permute-start = (bf16[16,8192]{1,0:T(8,128)(2,1)}, bf16[16,8192]{1,0:T(8,128)(2,1)S(1)}, u32[]{:S(2)}, u32[]{:S(2)}) collective-permute-start(bf16[16,8192]{1,0:T(8,128)(2,1)} %get-tuple-element.193), channel_id=1, source_target_pairs={{496,0},{0,16},{16,32},{32,48},{48,64},{64,80},{80,96},{96,112},{1... | collective-permute-start | bytes 786440 | tf_op jit(solution)/shard_map/while/body/eval_jaxpr/ppermute | solution.py:10
  581.7 17.2 %collective-permute-start = (bf16[16,8192]{1,0:T(8,128)(2,1)}, bf16[16,8192]{1,0:T(8,128)(2,1)S(1)}, u32[]{:S(2)}, u32[]{:S(2)}) collective-permute-start(bf16[16,8192]{1,0:T(8,128)(2,1)} %get-tuple-element.193), channel_id=1, source_target_pairs={{496,0},{0,16},{16,32},{32,48},{48,64},{64,80},{80,96},{96,112},{1... | collective-permute-start | bytes 786440 | tf_op jit(solution)/shard_map/while/body/eval_jaxpr/ppermute | solution.py:10
  601.0 16.4 %collective-permute-start = (bf16[16,8192]{1,0:T(8,128)(2,1)}, bf16[16,8192]{1,0:T(8,128)(2,1)S(1)}, u32[]{:S(2)}, u32[]{:S(2)}) collective-permute-start(bf16[16,8192]{1,0:T(8,128)(2,1)} %get-tuple-element.193), channel_id=1, source_target_pairs={{496,0},{0,16},{16,32},{32,48},{48,64},{64,80},{80,96},{96,112},{1... | collective-permute-start | bytes 786440 | tf_op jit(solution)/shard_map/while/body/eval_jaxpr/ppermute | solution.py:10
  619.3 18.0 %collective-permute-start = (bf16[16,8192]{1,0:T(8,128)(2,1)}, bf16[16,8192]{1,0:T(8,128)(2,1)S(1)}, u32[]{:S(2)}, u32[]{:S(2)}) collective-permute-start(bf16[16,8192]{1,0:T(8,128)(2,1)} %get-tuple-element.193), channel_id=1, source_target_pairs={{496,0},{0,16},{16,32},{32,48},{48,64},{64,80},{80,96},{96,112},{1... | collective-permute-start | bytes 786440 | tf_op jit(solution)/shard_map/while/body/eval_jaxpr/ppermute | solution.py:10
  639.3 17.2 %collective-permute-start = (bf16[16,8192]{1,0:T(8,128)(2,1)}, bf16[16,8192]{1,0:T(8,128)(2,1)S(1)}, u32[]{:S(2)}, u32[]{:S(2)}) collective-permute-start(bf16[16,8192]{1,0:T(8,128)(2,1)} %get-tuple-element.193), channel_id=1, source_target_pairs={{496,0},{0,16},{16,32},{32,48},{48,64},{64,80},{80,96},{96,112},{1... | collective-permute-start | bytes 786440 | tf_op jit(solution)/shard_map/while/body/eval_jaxpr/ppermute | solution.py:10
  658.5 13.5 %collective-permute-start = (bf16[16,8192]{1,0:T(8,128)(2,1)}, bf16[16,8192]{1,0:T(8,128)(2,1)S(1)}, u32[]{:S(2)}, u32[]{:S(2)}) collective-permute-start(bf16[16,8192]{1,0:T(8,128)(2,1)} %get-tuple-element.193), channel_id=1, source_target_pairs={{496,0},{0,16},{16,32},{32,48},{48,64},{64,80},{80,96},{96,112},{1... | collective-permute-start | bytes 786440 | tf_op jit(solution)/shard_map/while/body/eval_jaxpr/ppermute | solution.py:10
  (2 other events, 3.8 us)
where the time goes:
time: 677 us; the launch traced here: 676 us
  starting transfers between devices  272 us (40%)
  waiting for transfers between devices  257 us (38%)
  blocking collectives  67.8 us (10%)
  matrix products  46.5 us (7%)
  local copies, waits for them, and re-layouts  30.2 us (4%)
    ppermute x31, starting transfers between devices, from_behind(): return lax.ppermute(block, axis, route)  272 us
    ppermute x31, waiting for transfers between devices, from_behind(): return lax.ppermute(block, axis, route)  257 us
    psum x1, blocking collectives, local(): summed = lax.psum(joined, 'tensor')  67.8 us
    dot_general x32, matrix products, score_tile(): lax.dot_general(queries, incoming, (((1,), (1,)), ((), ())), preferred_el...  42.5 us
    while x31, local copies, waits for them, and re-layouts  21.8 us
  transfers between devices with their start and end apart: 31, of which 31 were waited for; matrix products, arithmetic and copies ran while one was open for 0% of the time, Pallas kernels for 0%

commit v1 on v0

v1 whole, which is shorter than its diff:
```python
import functools

import jax
import jax.numpy as jnp
from jax import lax
from jax.experimental import pallas as pl
from jax.experimental.pallas import tpu as pltpu
from jax.sharding import PartitionSpec as P

MESH = pl.DeviceIdType.MESH
F32, BF16 = jnp.float32, jnp.bfloat16
NT = (((1,), (1,)), ((), ()))
QROWS = 144


def wrap(v, n):
    return lax.rem(v + 4 * n, n)


def body(
    act, outg, proj_in, proj_out, ids, mask, queries, out,
    part1, recv1, sum1, recv2, act_low, grad_low, ids2, spread, perm, q_raw, q_perm, blocks, part, other,
    q_sem, own_sem, id_sem, s1_send, s1_recv, s2_send, s2_recv, s3_send, s3_recv, z_send, z_recv,
    line_send, line_recv, corner_send, corner_recv, o_send, o_recv,
):
    dp, tensor = lax.axis_index("dp"), lax.axis_index("tensor")
    x, zh, core = dp // 8, dp // 2 % 4, dp % 2
    zl, y = tensor // 4, tensor % 4
    twin = 1 - core
    z = zh * 4 + zl

    def device(dx=0, dy=0, dzh=0, dzl=0, c=core):
        return (
            (wrap(x + dx, 4) * 4 + wrap(zh + dzh, 4)) * 2 + c,
            wrap(zl + dzl, 4) * 4 + wrap(y + dy, 4),
        )

    def remote(src, dst, send, recv, dev):
        return pltpu.make_async_remote_copy(
            src_ref=src, dst_ref=dst, send_sem=send, recv_sem=recv, device_id=dev, device_id_type=MESH
        )

    barrier = pltpu.get_barrier_semaphore()
    peers = [device(dzh=a, dzl=b) for a in range(4) for b in range(4) if (a, b) != (0, 0)]
    peers += [device(dy=d, c=c) for d in (1, 2, 3) for c in (core, twin)]
    peers += [device(dx=d) for d in (1, 2, 3)] + [device(c=twin)]
    for peer in peers:
        pl.semaphore_signal(barrier, inc=1, device_id=peer, device_id_type=MESH)

    own_queries = pltpu.make_async_copy(queries.at[core], q_raw.at[core], own_sem)
    own_queries.start()

    masked = mask[...].astype(F32)
    for layer in range(2):
        a = lax.dot_general(proj_in[layer], act[layer], NT, preferred_element_type=F32)
        g = lax.dot_general(proj_out[layer], outg[layer], NT, preferred_element_type=F32) * masked
        for q in range(4):
            part1[layer, q, 0:16, :] = a[16 * q:16 * q + 16]
            for i in range(4):
                part1[layer, q, 16:32, 256 * i:256 * i + 256] = g[16 * i:16 * i + 16, 256 * q:256 * q + 256]

    pl.semaphore_wait(barrier, len(peers))

    copies1 = []
    for d in (2, 1, 3, 0):
        for other_core in (0, 1):
            if d or other_core:
                k = 2 * d + other_core
                c = twin if other_core else core
                copies1.append(remote(
                    part1.at[c, wrap(y + d, 4)], recv1.at[k], s1_send.at[k], s1_recv.at[k], device(dy=d, c=c)
                ))
    for copy in copies1:
        copy.start()
    ids2[core] = ids[...]
    id_copy = remote(ids, ids2.at[core], id_sem.at[0], id_sem.at[1], device(c=twin))
    id_copy.start()
    q_copy = remote(queries.at[twin], q_raw.at[core], q_sem.at[0], q_sem.at[1], device(c=twin))
    q_copy.start()

    rows = lax.broadcasted_iota(jnp.int32, (1024, 1024), 0)
    cols = lax.broadcasted_iota(jnp.int32, (1024, 1024), 1)
    place = rows // 16 % 4 * 256 + rows // 64 * 16 + rows % 16
    perm[...] = jnp.where(cols == place, 1.0, 0.0).astype(BF16)
    own_queries.wait()
    q_copy.wait()

    def reorder(step, carry):
        r, b = step // 4, lax.rem(step, 4)
        columns = pl.ds(pl.multiple_of(b * 1024, 1024), 1024)
        moved = jnp.dot(q_raw[r, :, columns], perm[...], preferred_element_type=F32).astype(BF16)
        for q in range(4):
            q_perm[q * 4 + b, r] = moved[:, 256 * q:256 * q + 256]
        return carry

    lax.fori_loop(0, 8, reorder, 0)

    for copy in copies1:
        copy.wait()
    for other_core in (0, 1):
        first = recv1[1] if other_core else part1[core, y]
        total = first + recv1[2 + other_core] + recv1[4 + other_core] + recv1[6 + other_core]
        row = twin if other_core else core
        for q in range(4):
            sum1[q, row] = total[:, 256 * q:256 * q + 256]

    copies2 = [
        remote(sum1.at[wrap(zl + d, 4)], recv2.at[d - 1], s2_send.at[d - 1], s2_recv.at[d - 1], device(dzl=d))
        for d in (2, 3, 1)
    ]
    for copy in copies2:
        copy.start()
    for copy in copies2:
        copy.wait()
    low = (sum1[zl] + recv2[0] + recv2[1] + recv2[2]).astype(BF16)
    act_low[zl] = low[:, 0:16]
    grad_low[y] = low[:, 16:32]
    copies3 = []
    for d in (1, 2, 3):
        copies3.append(remote(
            act_low.at[zl], act_low.at[zl], s3_send.at[0, d - 1], s3_recv.at[0, d - 1], device(dzl=d)
        ))
        copies3.append(remote(
            grad_low.at[y], grad_low.at[y], s3_send.at[1, d - 1], s3_recv.at[1, d - 1], device(dy=d)
        ))
    for copy in copies3:
        copy.start()
    id_copy.wait()
    for copy in copies3:
        copy.wait_send()
    for d in (1, 2, 3):
        remote(
            act_low.at[wrap(zl - d, 4)], act_low.at[wrap(zl - d, 4)],
            s3_send.at[0, d - 1], s3_recv.at[0, d - 1], device(dzl=d),
        ).wait_recv()
        remote(
            grad_low.at[wrap(y - d, 4)], grad_low.at[wrap(y - d, 4)],
            s3_send.at[1, d - 1], s3_recv.at[1, d - 1], device(dy=d),
        ).wait_recv()

    lane = lax.broadcasted_iota(jnp.int32, (16, 256), 1)
    repeat = jnp.where(lane % 16 == lax.broadcasted_iota(jnp.int32, (16, 256), 0), 1.0, 0.0).astype(BF16)
    for row in (0, 1):
        sums = jnp.zeros((256, 16), F32)
        for q in range(4):
            here = ids2[row][:, 256 * q:256 * q + 256]
            onehot = lax.broadcasted_iota(jnp.int32, (16, 256), 0) == here
            grads = grad_low[q, row].astype(F32)
            for i in range(16):
                spread[16 * i:16 * i + 16, :] = jnp.where(onehot, grads[i:i + 1], 0.0).astype(BF16)
            sums = sums + lax.dot_general(spread[...], act_low[q, row], NT, preferred_element_type=F32)
        wide = jnp.dot(sums.astype(BF16), repeat, preferred_element_type=F32)
        block = jnp.zeros((16, 256), F32)
        for i in range(16):
            block = block + jnp.where(lane // 16 == i, wide[16 * i:16 * i + 16], 0.0)
        blocks[y, x, z, 16 * row:16 * row + 16, :] = block.astype(BF16)

    z_copies = {}
    for a in (0, 1, 3, 2):
        for b in range(4):
            if (a, b) != (0, 0):
                g = (4 - a) % 4
                z_copies[g, b] = remote(
                    blocks.at[y, x, z], blocks.at[y, x, z], z_send.at[g, b], z_recv.at[g, b], device(dzh=a, dzl=b)
                )
                z_copies[g, b].start()

    def start_of(g):
        return wrap(zh + g, 4) * 4

    def line_copy(g, axis, d, back=False):
        run = pl.ds(start_of(g), 4)
        k = d - 1
        dev = device(dx=d) if axis == 0 else device(dy=d)
        sx = wrap(x - d, 4) if back and axis == 0 else x
        sy = wrap(y - d, 4) if back and axis == 1 else y
        ref = blocks.at[sy, sx, run]
        return remote(ref, ref, line_send.at[g, axis, k], line_recv.at[g, axis, k], dev)

    def corner_copy(g, axis, dx, dy, back=False):
        half = pl.ds(start_of(g) + 2 * axis, 2)
        sx, sy = wrap(x - dx, 4), wrap(y - dy, 4)
        if not back:
            sx, sy = (sx, y) if axis == 0 else (x, sy)
        ref = blocks.at[sy, sx, half]
        dev = device(dy=dy) if axis == 0 else device(dx=dx)
        k = (dx - 1) * 3 + dy - 1
        return remote(ref, ref, corner_send.at[g, axis, k], corner_recv.at[g, axis, k], dev)

    def from_z(g, b):
        ref = blocks.at[y, x, start_of(g) + wrap(zl - b, 4)]
        remote(ref, ref, z_send.at[g, b], z_recv.at[g, b], device(dzl=1)).wait_recv()

    def group_of(step):
        return jnp.where(step < 2, step, 5 - step)

    def score_copy(g):
        zone = wrap(zh + g, 4)
        return remote(part.at[twin, zone], other.at[zone], o_send.at[g], o_recv.at[g], device(c=twin))

    def advance(step, carry):
        @pl.when(step < 4)
        def _():
            g = group_of(step)

            @pl.when(step > 0)
            def _():
                from_z(g, 0)

            for b in (1, 2, 3):
                from_z(g, b)
            for d in (2, 1, 3):
                line_copy(g, 0, d).start()
                line_copy(g, 1, d).start()

        @pl.when((step >= 1) & (step < 5))
        def _():
            g = group_of(step - 1)
            for d in (1, 3, 2):
                line_copy(g, 0, d, back=True).wait_recv()
                for dy in (2, 1, 3):
                    corner_copy(g, 0, d, dy).start()
                line_copy(g, 1, d, back=True).wait_recv()
                for dx in (2, 1, 3):
                    corner_copy(g, 1, dx, d).start()

        @pl.when(step >= 2)
        def _():
            g = group_of(step - 2)
            for dx in (1, 2, 3):
                for dy in (1, 2, 3):
                    corner_copy(g, 0, dx, dy, back=True).wait_recv()
                    corner_copy(g, 1, dx, dy, back=True).wait_recv()
            first = start_of(g)
            scores = jnp.zeros((2 * QROWS, 128), F32)
            for yy in range(4):
                for b in range(4):
                    lhs = q_perm[yy * 4 + b].reshape(2 * QROWS, 256)
                    rhs = blocks[yy, :, first + b].reshape(128, 256)
                    scores = scores + lax.dot_general(lhs, rhs, NT, preferred_element_type=F32)
            zone = wrap(zh + g, 4)
            part[0, zone] = scores[:QROWS]
            part[1, zone] = scores[QROWS:]
            score_copy(g).start()

        return carry

    lax.fori_loop(0, 6, advance, 0)

    def finish(step, carry):
        for axis in (0, 1):
            for d in (1, 2, 3):
                line_copy(step, axis, d).wait_send()
                for e in (1, 2, 3):
                    corner_copy(step, axis, d, e).wait_send()
        zone = wrap(zh + step, 4)
        ref = other.at[zone]
        remote(part.at[twin, zone], ref, o_send.at[step], o_recv.at[step], device(c=twin)).wait()
        return carry

    lax.fori_loop(0, 4, finish, 0)
    for copy in z_copies.values():
        copy.wait_send()

    sums = [part[core, g] + other[g] for g in range(4)]
    for xx in range(4):
        pieces = [sums[g][:136, 32 * xx:32 * xx + 32] for g in range(4)]
        out[:, 128 * xx:128 * xx + 128] = jnp.concatenate(pieces, axis=1)


def local(activations, out_grads, proj_in, proj_out, example_ids, loss_mask, query_grads):
    queries = jnp.pad(jnp.transpose(query_grads, (1, 0, 2)), ((0, 0), (0, QROWS - 136), (0, 0)))
    vmem = pl.BlockSpec(memory_space=pltpu.VMEM)
    dma = pltpu.SemaphoreType.DMA
    return pl.pallas_call(
        body,
        out_shape=jax.ShapeDtypeStruct((136, 512), F32),
        in_specs=[vmem] * 6 + [pl.BlockSpec(memory_space=pl.ANY)],
        out_specs=vmem,
        scratch_shapes=[
            pltpu.VMEM((2, 4, 32, 1024), F32),
            pltpu.VMEM((8, 32, 1024), F32),
            pltpu.VMEM((4, 2, 32, 256), F32),
            pltpu.VMEM((3, 2, 32, 256), F32),
            pltpu.VMEM((4, 2, 16, 256), BF16),
            pltpu.VMEM((4, 2, 16, 256), BF16),
            pltpu.VMEM((2, 1, 1024), jnp.int32),
            pltpu.VMEM((256, 256), BF16),
            pltpu.VMEM((1024, 1024), BF16),
            pltpu.VMEM((2, QROWS, 4096), BF16),
            pltpu.VMEM((16, 2, QROWS, 256), BF16),
            pltpu.VMEM((4, 4, 16, 32, 256), BF16),
            pltpu.VMEM((2, 4, QROWS, 128), F32),
            pltpu.VMEM((4, QROWS, 128), F32),
            dma((2,)), dma, dma((2,)), dma((8,)), dma((8,)), dma((3,)), dma((3,)), dma((2, 3)), dma((2, 3)),
            dma((4, 4)), dma((4, 4)), dma((4, 2, 3)), dma((4, 2, 3)), dma((4, 2, 9)), dma((4, 2, 9)),
            dma((4,)), dma((4,)),
        ],
        compiler_params=pltpu.CompilerParams(
            collective_id=0, has_side_effects=True, vmem_limit_bytes=48 * 2**20
        ),
        name="scores",
    )(activations, out_grads, proj_in, proj_out, example_ids, loss_mask, queries)


def solution(mesh):
    in_specs = (
        P(None, "dp", "tensor"),
        P(None, "dp", "tensor"),
        P(None, None, "tensor"),
        P(None, None, "tensor"),
        P("dp", None),
        P("dp", None),
        P(("dp", "tensor"), None, None),
    )
    out_specs = P(("dp", "tensor"), None)
    return jax.shard_map(local, mesh=mesh, in_specs=in_specs, out_specs=out_specs, check_vma=False)
```

time: 677 us -> 90.9 us (0.13)
  the two profiles are of different devices: /device:TPU:45 before, /device:TPU:1 now
where the time goes in v1:
time: 90.9 us; the launch traced here: 90.7 us
  Pallas kernels  85.4 us (94%)
  local copies, waits for them, and re-layouts  5.23 us (6%)
    pallas_call x1, Pallas kernels, local(): pl.pallas_call(body, out_shape=jax.ShapeDtypeStruct((136, 512), F32), in_...  85.4 us
    unnamed x14, local copies, waits for them, and re-layouts  4.97 us

profile of v1, /device:TPU:1, one launch (start us, length us, event | category | flops | bytes accessed | tf_op | source)
XLA Modules:
  0.0 90.7 jit_solution(13483504853237371066)
XLA Ops:
  0.0 3.0 %copy.10 = bf16[136,2,4096]{2,0,1:T(8,128)(2,1)S(1)} copy(bf16[136,2,4096]{2,1,0:T(2,128)(2,1)} %param.13) | data formatting | bytes 4456448 | tf_op args[6]
  3.0 0.0 copy-start
  3.0 0.0 copy-start.1
  3.0 0.0 copy-start.2
  3.1 0.0 copy-start.3
  3.1 0.0 copy-start.4
  3.1 0.0 copy-start.5
  3.1 0.3 pad.4.queries
  3.4 0.9 copy-done
  4.2 0.3 copy-done.1
  4.6 0.0 copy-done.2
  4.6 0.0 copy-done.3
  4.6 0.0 copy-done.4
  4.6 0.0 copy-done.5
  4.6 85.4 %scores.1 = f32[136,512]{1,0:T(8,128)S(1)} custom-call(bf16[2,1024,256]{2,1,0:T(8,128)(2,1)S(1)} %copy-done, bf16[2,1024,256]{2,1,0:T(8,128)(2,1)S(1)} %copy-done.1, bf16[2,64,256]{2,1,0:T(8,128)(2,1)S(1)} %copy-done.2, bf16[2,64,256]{2,1,0:T(8,128)(2,1)S(1)} %copy-done.3, s32[1,1024]{1,0:T(1,128)S(1)} %copy-done.4, s32[1,1024]{1,0:T(1,128)S(1)} %copy-done.5, ...), custom_call_target="tpu_custom_call" | custom-call | tf_op jit(solution)/shard_map/scores/pallas_call | solution.py:275
  90.0 0.7 copy.12
Async XLA Ops:
  3.0 1.2 %copy-start = (bf16[2,1024,256]{2,1,0:T(8,128)(2,1)S(1)}, bf16[2,1024,256]{2,1,0:T(8,128)(2,1)}, u32[]{:S(2)}) copy-start(bf16[2,1024,256]{2,1,0:T(8,128)(2,1)} %act.1) | copy-start | bytes 3145732
  3.0 1.5 %copy-start.1 = (bf16[2,1024,256]{2,1,0:T(8,128)(2,1)S(1)}, bf16[2,1024,256]{2,1,0:T(8,128)(2,1)}, u32[]{:S(2)}) copy-start(bf16[2,1024,256]{2,1,0:T(8,128)(2,1)} %outg.1) | copy-start | bytes 3145732
  3.0 1.5 %copy-start.2 = (bf16[2,64,256]{2,1,0:T(8,128)(2,1)S(1)}, bf16[2,64,256]{2,1,0:T(8,128)(2,1)}, u32[]{:S(2)}) copy-start(bf16[2,64,256]{2,1,0:T(8,128)(2,1)} %proj_in.1) | copy-start | bytes 196612
  3.1 1.5 %copy-start.3 = (bf16[2,64,256]{2,1,0:T(8,128)(2,1)S(1)}, bf16[2,64,256]{2,1,0:T(8,128)(2,1)}, u32[]{:S(2)}) copy-start(bf16[2,64,256]{2,1,0:T(8,128)(2,1)} %proj_out.1) | copy-start | bytes 196612
  3.1 1.5 %copy-start.4 = (s32[1,1024]{1,0:T(1,128)S(1)}, s32[1,1024]{1,0:T(1,128)}, u32[]{:S(2)}) copy-start(s32[1,1024]{1,0:T(1,128)} %ids.1) | copy-start | bytes 12292
  3.1 1.5 %copy-start.5 = (s32[1,1024]{1,0:T(1,128)S(1)}, s32[1,1024]{1,0:T(1,128)}, u32[]{:S(2)}) copy-start(s32[1,1024]{1,0:T(1,128)} %mask.1) | copy-start | bytes 12292

commit v2 on v1

v2 whole, which is shorter than its diff:
```python
import jax
import jax.numpy as jnp
from jax import lax
from jax.experimental import pallas as pl
from jax.experimental.pallas import tpu as pltpu
from jax.sharding import PartitionSpec as P

MESH = pl.DeviceIdType.MESH
F32, BF16 = jnp.float32, jnp.bfloat16
NT = (((1,), (1,)), ((), ()))
QROWS = 144


def wrap(v, n):
    return lax.rem(v + 4 * n, n)


def body(
    act_hbm, outg_hbm, in_hbm, out_hbm, ids_hbm, mask_hbm, queries, out,
    act, outg, proj_in, proj_out, ids, mask, q_pairs, q_wide, q_twin,
    part1, relay, mixed, recv1, sum1, recv2, act_low, grad_low, ids2, spread, perm, q_raw, q_perm, blocks, part, other,
    vouch, in_sem, q_sem, id_sem, r_send, r_recv, s1_send, s1_recv, s2_send, s2_recv, s3_send, s3_recv, z_send, z_recv,
    xy_send, xy_recv, o_send, o_recv,
):
    dp, tensor = lax.axis_index("dp"), lax.axis_index("tensor")
    x, zh, core = dp // 8, dp // 2 % 4, dp % 2
    zl, y = tensor // 4, tensor % 4
    twin = 1 - core
    z = zh * 4 + zl

    def device(dx=0, dy=0, dzh=0, dzl=0, c=core):
        return (
            (wrap(x + dx, 4) * 4 + wrap(zh + dzh, 4)) * 2 + c,
            wrap(zl + dzl, 4) * 4 + wrap(y + dy, 4),
        )

    def remote(src, dst, send, recv, dev):
        return pltpu.make_async_remote_copy(
            src_ref=src, dst_ref=dst, send_sem=send, recv_sem=recv, device_id=dev, device_id_type=MESH
        )

    def along(d):
        to = lax.rem(z + 16 + d, 16)
        return ((x * 4 + to // 4) * 2 + core, lax.rem(to, 4) * 4 + y)

    barrier = pltpu.get_barrier_semaphore()
    peers = [along(d) for d in (4, -4, 3, -3, 2, -2, 1, -1)]
    peers += [device(dy=d, c=c) for d in (1, 3) for c in (core, twin)]
    peers += [device(dy=2), device(dx=1), device(dx=2), device(dx=3), device(c=twin)]
    for peer in peers:
        pl.semaphore_signal(barrier, inc=1, device_id=peer, device_id_type=MESH)

    loads = [
        pltpu.make_async_copy(src, dst, in_sem.at[k])
        for k, (src, dst) in enumerate([
            (in_hbm, proj_in), (act_hbm, act), (out_hbm, proj_out), (mask_hbm, mask), (outg_hbm, outg),
            (ids_hbm, ids), (queries, q_pairs),
        ])
    ]
    for load in loads:
        load.start()

    loads[0].wait()
    loads[1].wait()

    def project_act(layer, carry):
        a = lax.dot_general(proj_in[layer], act[layer], NT, preferred_element_type=F32)
        for q in range(4):
            part1[q, layer, 0] = a[16 * q:16 * q + 16]
        return carry

    lax.fori_loop(0, 2, project_act, 0)
    for load in loads[2:5]:
        load.wait()

    def project_grad(layer, carry):
        g = lax.dot_general(proj_out[layer], outg[layer], NT, preferred_element_type=F32) * mask[...].astype(F32)
        for q in range(4):
            for i in range(4):
                part1[q, layer, 1, :, 256 * i:256 * i + 256] = g[16 * i:16 * i + 16, 256 * q:256 * q + 256]
        return carry

    lax.fori_loop(0, 2, project_grad, 0)

    pl.semaphore_wait(barrier, len(peers))
    pl.semaphore_signal(vouch.at[0], inc=1, device_id=along(4), device_id_type=MESH)
    pl.semaphore_signal(vouch.at[1], inc=1, device_id=along(-4), device_id_type=MESH)

    def relay_copy(half):
        d = 3 if half else 1
        return remote(
            part1.at[wrap(y + 2, 4), :, half], relay.at[half], r_send.at[half], r_recv.at[half], device(dy=d)
        )

    def plain_copy(half, cross):
        d = 1 if half else 3
        c = twin if cross else core
        return remote(
            part1.at[wrap(y + d, 4), c, half], recv1.at[cross, 0, half], s1_send.at[cross, 0, half],
            s1_recv.at[cross, 0, half], device(dy=d, c=c),
        )

    def mixed_copy(half, cross):
        d = 3 if half else 1
        c = twin if cross else core
        return remote(
            mixed.at[half, c], recv1.at[cross, 1, half], s1_send.at[cross, 1, half],
            s1_recv.at[cross, 1, half], device(dy=d, c=c),
        )

    twin_copy = remote(part1.at[y, twin], recv1.at[1, 2], s1_send.at[0, 2, 0], s1_recv.at[0, 2, 0], device(c=twin))
    both = [(half, cross) for cross in (0, 1) for half in (0, 1)]
    for half in (0, 1):
        relay_copy(half).start()
    for half, cross in both:
        plain_copy(half, cross).start()
    twin_copy.start()
    loads[5].wait()
    ids2[core] = ids[...]
    id_copy = remote(ids, ids2.at[core], id_sem.at[0], id_sem.at[1], device(c=twin))
    id_copy.start()

    loads[6].wait()

    def widen(step, carry):
        rows = pl.ds(pl.multiple_of(step * 512, 512), 512)
        q_wide[rows, :] = q_pairs[rows, :].astype(F32)
        return carry

    lax.fori_loop(0, 17, widen, 0)
    filler = jnp.zeros((QROWS - 136, 128), F32)

    def pick(layer, dst):
        def one(step, carry):
            rows = q_wide[pl.ds(2 * step + layer, 136, stride=64), :]
            dst[:, pl.ds(pl.multiple_of(step * 128, 128), 128)] = jnp.concatenate([rows, filler], axis=0).astype(BF16)
            return carry

        lax.fori_loop(0, 32, one, 0)

    pick(twin, q_twin)
    q_copy = remote(q_twin, q_raw.at[core], q_sem.at[0], q_sem.at[1], device(c=twin))
    q_copy.start()

    for half in (0, 1):
        relay_copy(half).wait()
        mixed[half] = relay[half] + part1[wrap(y + (3 if half else 1), 4), :, half]
        for cross in (0, 1):
            mixed_copy(half, cross).start()

    pick(core, q_raw.at[core])
    row = lax.broadcasted_iota(jnp.int32, (512, 1), 0)
    place = lax.rem(row // 16, 4) * 128 + row // 64 * 16 + lax.rem(row, 16)
    perm[...] = jnp.where(lax.broadcasted_iota(jnp.int32, (512, 512), 1) == place, 1.0, 0.0).astype(BF16)

    for half, cross in both:
        plain_copy(half, cross).wait()
        mixed_copy(half, cross).wait()
    twin_copy.wait()
    for cross in (0, 1):
        mine = recv1[1, 2] if cross else part1[y, core]
        total = mine + recv1[cross, 0] + recv1[cross, 1]
        for q in range(4):
            sum1[q, twin if cross else core] = total[:, :, 256 * q:256 * q + 256].reshape(32, 256)

    copies2 = [
        remote(sum1.at[wrap(zl + d, 4)], recv2.at[d - 1], s2_send.at[d - 1], s2_recv.at[d - 1], device(dzl=d))
        for d in (2, 3, 1)
    ]
    for copy in copies2:
        copy.start()
    q_copy.wait()

    def reorder(step, carry):
        b, half = step // 2, lax.rem(step, 2)
        columns = pl.ds(pl.multiple_of(step * 512, 512), 512)
        into = pl.ds(pl.multiple_of(half * 128, 128), 128)
        lhs = q_raw[:, :, columns].reshape(2 * QROWS, 512)
        moved = jnp.dot(lhs, perm[...], preferred_element_type=F32).astype(BF16).reshape(2, QROWS, 512)
        for q in range(4):
            q_perm[q * 4 + b, :, :, into] = moved[:, :, 128 * q:128 * q + 128]
        return carry

    lax.fori_loop(0, 8, reorder, 0)
    for copy in copies2:
        copy.wait()
    low = (sum1[zl] + recv2[0] + recv2[1] + recv2[2]).astype(BF16)
    act_low[zl] = low[:, 0:16]
    grad_low[y] = low[:, 16:32]
    copies3 = []
    for d in (1, 2, 3):
        copies3.append(remote(
            act_low.at[zl], act_low.at[zl], s3_send.at[0, d - 1], s3_recv.at[0, d - 1], device(dzl=d)
        ))
        copies3.append(remote(
            grad_low.at[y], grad_low.at[y], s3_send.at[1, d - 1], s3_recv.at[1, d - 1], device(dy=d)
        ))
    for copy in copies3:
        copy.start()
    id_copy.wait()
    for copy in copies3:
        copy.wait_send()
    for d in (1, 2, 3):
        remote(
            act_low.at[wrap(zl - d, 4)], act_low.at[wrap(zl - d, 4)],
            s3_send.at[0, d - 1], s3_recv.at[0, d - 1], device(dzl=d),
        ).wait_recv()
        remote(
            grad_low.at[wrap(y - d, 4)], grad_low.at[wrap(y - d, 4)],
            s3_send.at[1, d - 1], s3_recv.at[1, d - 1], device(dy=d),
        ).wait_recv()

    lane = lax.broadcasted_iota(jnp.int32, (16, 256), 1)
    repeat = jnp.where(lane % 16 == lax.broadcasted_iota(jnp.int32, (16, 256), 0), 1.0, 0.0).astype(BF16)

    def form(row, carry):
        def add(q, sums):
            here = ids2[row, :, pl.ds(pl.multiple_of(q * 256, 256), 256)]
            onehot = lax.broadcasted_iota(jnp.int32, (16, 256), 0) == here
            grads = grad_low[q, row].astype(F32)
            for i in range(16):
                spread[16 * i:16 * i + 16, :] = jnp.where(onehot, grads[i:i + 1], 0.0).astype(BF16)
            return sums + lax.dot_general(spread[...], act_low[q, row], NT, preferred_element_type=F32)

        sums = lax.fori_loop(0, 4, add, jnp.zeros((256, 16), F32))
        wide = jnp.dot(sums.astype(BF16), repeat, preferred_element_type=F32)
        block = jnp.zeros((16, 256), F32)
        for i in range(16):
            block = block + jnp.where(lane // 16 == i, wide[16 * i:16 * i + 16], 0.0)
        blocks[0, 0, 0, 0, 0, pl.ds(pl.multiple_of(16 * row, 16), 16), :] = block.astype(BF16)
        return carry

    lax.fori_loop(0, 2, form, 0)

    slot_of = (0, 1, 3, 2)

    pl.semaphore_wait(vouch.at[0], 1)
    pl.semaphore_wait(vouch.at[1], 1)
    z_copies = {}
    for a in (0, 1, 3, 2):
        for b in (1, 3, 2, 0):
            if (a, b) != (0, 0):
                slot, k = slot_of[(4 - a) % 4], (4 - b) % 4
                z_copies[slot, k] = remote(
                    blocks.at[0, 0, 0, 0, 0], blocks.at[slot, k // 2, 0, 0, k % 2], z_send.at[slot, k],
                    z_recv.at[slot, k], device(dzh=a, dzl=b),
                )
                z_copies[slot, k].start()

    ways = [device(dx=1), device(dx=3), device(dy=1), device(dy=3), device(dx=2), device(dy=2)]

    def stage(slot, n):
        at = lambda *k: blocks.at[(slot,) + k]
        all_, rest = slice(None), pl.ds(1, 3)
        if slot == 3 and n == 0:
            src = [at(all_, 0, 0)] * 6
            dst = [at(all_, 0, 3), at(all_, 0, 1), at(all_, 3, 0), at(all_, 1, 0), at(all_, 0, 2), at(all_, 2, 0)]
        elif slot == 3:
            src = [at(1, rest, 0)] * 2 + [at(0, 0, rest)] * 2 + [at(1, rest, 0), at(0, 0, rest)]
            dst = [at(1, rest, 3), at(1, rest, 1), at(0, 3, rest), at(0, 1, rest), at(1, rest, 2), at(0, 2, rest)]
        elif n == 0:
            src = [at(all_, 0, 0)] * 4
            dst = [at(all_, 0, 3), at(all_, 0, 1), at(all_, 3, 0), at(all_, 1, 0)]
        elif n == 1:
            src = [at(0, 0, 3), at(1, 0, 1), at(0, 3, 0), at(1, 1, 0)]
            dst = [at(0, 0, 2), at(1, 0, 2), at(0, 2, 0), at(1, 2, 0)]
        elif n == 2:
            src = [at(1, rest, 0)] * 2 + [at(0, 0, rest)] * 2
            dst = [at(1, rest, 3), at(1, rest, 1), at(0, 3, rest), at(0, 1, rest)]
        else:
            src = [at(1, rest, 3, 0), at(1, rest, 1, 1), at(0, 3, rest, 0), at(0, 1, rest, 1)]
            dst = [at(1, rest, 2, 0), at(1, rest, 2, 1), at(0, 2, rest, 0), at(0, 2, rest, 1)]
        return [
            remote(src[k], dst[k], xy_send.at[slot, n, k], xy_recv.at[slot, n, k], ways[k])
            for k in range(len(src))
        ]

    count = (4, 4, 4, 2)
    stages = {(slot, n): stage(slot, n) for slot in range(4) for n in range(count[slot])}
    score_copies = [
        remote(part.at[twin, slot], other.at[slot], o_send.at[slot], o_recv.at[slot], device(c=twin))
        for slot in range(4)
    ]

    def go(slot, n):
        if n == 0:
            for k in range(4):
                if (slot, k) != (0, 0):
                    z_copies[slot, k].wait_recv()
        else:
            for copy in stages[slot, n - 1]:
                copy.wait_recv()
        if n < count[slot]:
            for copy in stages[slot, n]:
                copy.start()

    def score(slot):
        def add(dy, scores):
            for k in range(4):
                lhs = q_perm[wrap(y + dy, 4) * 4 + wrap(zl + k, 4)].reshape(2 * QROWS, 256)
                rhs = blocks[slot, k // 2, dy, :, k % 2].reshape(128, 256)
                scores = scores + lax.dot_general(lhs, rhs, NT, preferred_element_type=F32)
            return scores

        scores = lax.fori_loop(0, 4, add, jnp.zeros((2 * QROWS, 128), F32))
        part[0, slot] = scores[:QROWS]
        part[1, slot] = scores[QROWS:]
        score_copies[slot].start()

    order = [
        (0, 0), (0, 1), (1, 0), (2, 0), (0, 2), (1, 1), (2, 1), (0, 3), (3, 0), (1, 2), (2, 2), (0, 4), (3, 1),
        (1, 3), (2, 3), (1, 4), (2, 4), (3, 2),
    ]
    for slot, n in order:
        go(slot, n)
        if n == count[slot]:
            score(slot)

    for copy in z_copies.values():
        copy.wait_send()
    for copies in stages.values():
        for copy in copies:
            copy.wait_send()
    for copy in score_copies:
        copy.wait()

    sums = [part[core, slot_of[r]] + other[slot_of[r]] for r in range(4)]
    for dx in range(4):
        pieces = [sums[r][:136, 32 * dx:32 * dx + 32] for r in range(4)]
        piece = pltpu.roll(jnp.concatenate(pieces, axis=1), zh * 32, 1)
        out[:, pl.ds(pl.multiple_of(wrap(x + dx, 4) * 128, 128), 128)] = piece


def local(activations, out_grads, proj_in, proj_out, example_ids, loss_mask, query_grads):
    queries = query_grads.reshape(136, 2, 32, 128).transpose(0, 2, 1, 3).reshape(136 * 64, 128)
    dma = pltpu.SemaphoreType.DMA
    return pl.pallas_call(
        body,
        out_shape=jax.ShapeDtypeStruct((136, 512), F32),
        in_specs=[pl.BlockSpec(memory_space=pl.ANY)] * 7,
        out_specs=pl.BlockSpec(memory_space=pltpu.VMEM),
        scratch_shapes=[
            pltpu.VMEM((2, 1024, 256), BF16),
            pltpu.VMEM((2, 1024, 256), BF16),
            pltpu.VMEM((2, 64, 256), BF16),
            pltpu.VMEM((2, 64, 256), BF16),
            pltpu.VMEM((1, 1024), jnp.int32),
            pltpu.VMEM((1, 1024), jnp.int32),
            pltpu.VMEM((136 * 64, 128), BF16),
            pltpu.VMEM((136 * 64, 128), F32),
            pltpu.VMEM((QROWS, 4096), BF16),
            pltpu.VMEM((4, 2, 2, 16, 1024), F32),
            pltpu.VMEM((2, 2, 16, 1024), F32),
            pltpu.VMEM((2, 2, 16, 1024), F32),
            pltpu.VMEM((2, 3, 2, 16, 1024), F32),
            pltpu.VMEM((4, 2, 32, 256), F32),
            pltpu.VMEM((3, 2, 32, 256), F32),
            pltpu.VMEM((4, 2, 16, 256), BF16),
            pltpu.VMEM((4, 2, 16, 256), BF16),
            pltpu.VMEM((2, 1, 1024), jnp.int32),
            pltpu.VMEM((256, 256), BF16),
            pltpu.VMEM((512, 512), BF16),
            pltpu.VMEM((2, QROWS, 4096), BF16),
            pltpu.VMEM((16, 2, QROWS, 256), BF16),
            pltpu.VMEM((4, 2, 4, 4, 2, 32, 256), BF16),
            pltpu.VMEM((2, 4, QROWS, 128), F32),
            pltpu.VMEM((4, QROWS, 128), F32),
            pltpu.SemaphoreType.REGULAR((2,)), dma((7,)), dma((2,)), dma((2,)), dma((2,)), dma((2,)), dma((2, 3, 2)), dma((2, 3, 2)),
            dma((3,)), dma((3,)), dma((2, 3)), dma((2, 3)), dma((4, 4)), dma((4, 4)),
            dma((4, 4, 6)), dma((4, 4, 6)), dma((4,)), dma((4,)),
        ],
        compiler_params=pltpu.CompilerParams(
            collective_id=0, has_side_effects=True, vmem_limit_bytes=56 * 2**20
        ),
        name="scores",
    )(activations, out_grads, proj_in, proj_out, example_ids, loss_mask, queries)


def solution(mesh):
    in_specs = (
        P(None, "dp", "tensor"),
        P(None, "dp", "tensor"),
        P(None, None, "tensor"),
        P(None, None, "tensor"),
        P("dp", None),
        P("dp", None),
        P(("dp", "tensor"), None, None),
    )
    out_specs = P(("dp", "tensor"), None)
    return jax.shard_map(local, mesh=mesh, in_specs=in_specs, out_specs=out_specs, check_vma=False)
```

time: 90.9 us -> 83.7 us (0.921)
  Pallas kernels: 85.4 us -> 81.8 us
  local copies, waits for them, and re-layouts: 5.23 us -> 1.68 us
    pallas_call x1, Pallas kernels: 85.4 us -> 81.8 us  [local(): pl.pallas_call(body, out_shape=jax.ShapeDtypeStruct((136, 512), F32), in_...]
    unnamed x14 -> x1, local copies, waits for them, and re-layouts: 4.97 us -> 1.68 us
where the time goes in v2:
time: 83.7 us; the launch traced here: 83.5 us
  Pallas kernels  81.8 us (98%)
  local copies, waits for them, and re-layouts  1.68 us (2%)
    pallas_call x1, Pallas kernels, local(): pl.pallas_call(body, out_shape=jax.ShapeDtypeStruct((136, 512), F32), in_...  81.8 us
    unnamed x1, local copies, waits for them, and re-layouts  1.68 us

profile of v2, /device:TPU:1, one launch (start us, length us, event | category | flops | bytes accessed | tf_op | source)
XLA Modules:
  0.0 83.5 jit_solution(2721776303288065086)
XLA Ops:
  0.0 81.8 %scores.1 = f32[136,512]{1,0:T(8,128)} custom-call(bf16[2,1024,256]{2,1,0:T(8,128)(2,1)} %act_hbm.1, bf16[2,1024,256]{2,1,0:T(8,128)(2,1)} %outg_hbm.1, bf16[2,64,256]{2,1,0:T(8,128)(2,1)} %in_hbm.1, bf16[2,64,256]{2,1,0:T(8,128)(2,1)} %out_hbm.1, s32[1,1024]{1,0:T(1,128)} %ids_hbm.1, s32[1,1024]{1,0:T(1,128)} %mask_hbm.1, bf16[8704,128]{1,0:T(8,128)(2,1)} %bitcast.5), custom_call_target="tpu_custom_call" | custom-call | tf_op jit(solution)/shard_map/scores/pallas_call | solution.py:337
  81.8 1.7 %copy.10 = f32[136,512]{1,0:T(8,128)} copy(f32[136,512]{1,0:T(8,128)} %scores.1) | data formatting | bytes 557056

commit v3 on v2

v3 whole, which is shorter than its diff:
```python
import jax
import jax.numpy as jnp
from jax import lax
from jax.experimental import pallas as pl
from jax.experimental.pallas import tpu as pltpu
from jax.sharding import PartitionSpec as P

MESH = pl.DeviceIdType.MESH
F32, BF16 = jnp.float32, jnp.bfloat16
NT = (((1,), (1,)), ((), ()))
QROWS = 144


def wrap(v, n):
    return lax.rem(v + 4 * n, n)


def body(
    act_hbm, outg_hbm, in_hbm, out_hbm, ids_hbm, mask_hbm, queries, out,
    act, outg, proj_in, proj_out, ids, mask, q_pairs, q_wide, q_twin,
    part1, relay, mixed, recv1, sum1, recv2, act_low, grad_low, ids2, spread, perm, q_raw, q_perm, blocks, part, other,
    in_sem, q_sem, id_sem, r_send, r_recv, s1_send, s1_recv, s2_send, s2_recv, s3_send, s3_recv, z1_send, z1_recv, z2_send, z2_recv,
    xy_send, xy_recv, o_send, o_recv,
):
    dp, tensor = lax.axis_index("dp"), lax.axis_index("tensor")
    x, zh, core = dp // 8, dp // 2 % 4, dp % 2
    zl, y = tensor // 4, tensor % 4
    twin = 1 - core
    z = zh * 4 + zl

    def device(dx=0, dy=0, dzh=0, dzl=0, c=core):
        return (
            (wrap(x + dx, 4) * 4 + wrap(zh + dzh, 4)) * 2 + c,
            wrap(zl + dzl, 4) * 4 + wrap(y + dy, 4),
        )

    def remote(src, dst, send, recv, dev):
        return pltpu.make_async_remote_copy(
            src_ref=src, dst_ref=dst, send_sem=send, recv_sem=recv, device_id=dev, device_id_type=MESH
        )

    def along(d):
        to = lax.rem(z + 16 + d, 16)
        return ((x * 4 + to // 4) * 2 + core, lax.rem(to, 4) * 4 + y)

    barrier = pltpu.get_barrier_semaphore()
    peers = [along(d) for d in (4, -4, 3, -3, 2, -2, 1, -1)]
    peers += [device(dy=d, c=c) for d in (1, 3) for c in (core, twin)]
    peers += [device(dy=2), device(dx=1), device(dx=3), device(c=twin)]
    for peer in peers:
        pl.semaphore_signal(barrier, inc=1, device_id=peer, device_id_type=MESH)

    loads = [
        pltpu.make_async_copy(src, dst, in_sem.at[k])
        for k, (src, dst) in enumerate([
            (in_hbm, proj_in), (act_hbm, act), (out_hbm, proj_out), (mask_hbm, mask), (outg_hbm, outg),
            (ids_hbm, ids), (queries, q_pairs),
        ])
    ]
    for load in loads:
        load.start()

    loads[0].wait()
    loads[1].wait()

    def project_act(layer, carry):
        a = lax.dot_general(proj_in[layer], act[layer], NT, preferred_element_type=F32)
        for q in range(4):
            part1[q, layer, 0] = a[16 * q:16 * q + 16]
        return carry

    lax.fori_loop(0, 2, project_act, 0)
    pl.semaphore_wait(barrier, len(peers))

    def relay_copy(half):
        d = 3 if half else 1
        return remote(
            part1.at[wrap(y + 2, 4), :, half], relay.at[half], r_send.at[half], r_recv.at[half], device(dy=d)
        )

    def plain_copy(half, cross):
        d = 1 if half else 3
        c = twin if cross else core
        return remote(
            part1.at[wrap(y + d, 4), c, half], recv1.at[cross, 0, half], s1_send.at[cross, 0, half],
            s1_recv.at[cross, 0, half], device(dy=d, c=c),
        )

    def mixed_copy(half, cross):
        d = 3 if half else 1
        c = twin if cross else core
        return remote(
            mixed.at[half, c], recv1.at[cross, 1, half], s1_send.at[cross, 1, half],
            s1_recv.at[cross, 1, half], device(dy=d, c=c),
        )

    def twin_copy(half):
        return remote(
            part1.at[y, twin, half], recv1.at[1, 2, half], s1_send.at[0, 2, half], s1_recv.at[0, 2, half],
            device(c=twin),
        )

    relay_copy(0).start()
    for cross in (0, 1):
        plain_copy(0, cross).start()
    twin_copy(0).start()
    for load in loads[2:5]:
        load.wait()

    def project_grad(layer, carry):
        g = lax.dot_general(proj_out[layer], outg[layer], NT, preferred_element_type=F32) * mask[...].astype(F32)
        for q in range(4):
            for i in range(4):
                part1[q, layer, 1, :, 256 * i:256 * i + 256] = g[16 * i:16 * i + 16, 256 * q:256 * q + 256]
        return carry

    lax.fori_loop(0, 2, project_grad, 0)

    relay_copy(1).start()
    for cross in (0, 1):
        plain_copy(1, cross).start()
    twin_copy(1).start()
    loads[5].wait()
    ids2[core] = ids[...]
    id_copy = remote(ids, ids2.at[core], id_sem.at[0], id_sem.at[1], device(c=twin))
    id_copy.start()

    loads[6].wait()

    def widen(step, carry):
        rows = pl.ds(pl.multiple_of(step * 512, 512), 512)
        q_wide[rows, :] = q_pairs[rows, :].astype(F32)
        return carry

    lax.fori_loop(0, 17, widen, 0)
    filler = jnp.zeros((QROWS - 136, 128), F32)

    def pick(layer, dst):
        def one(step, carry):
            rows = q_wide[pl.ds(2 * step + layer, 136, stride=64), :]
            dst[:, pl.ds(pl.multiple_of(step * 128, 128), 128)] = jnp.concatenate([rows, filler], axis=0).astype(BF16)
            return carry

        lax.fori_loop(0, 32, one, 0)

    pick(twin, q_twin)
    q_copy = remote(q_twin, q_raw.at[core], q_sem.at[0], q_sem.at[1], device(c=twin))
    q_copy.start()

    for half in (0, 1):
        relay_copy(half).wait()
        mixed[half] = relay[half] + part1[wrap(y + (3 if half else 1), 4), :, half]
        for cross in (0, 1):
            mixed_copy(half, cross).start()

    pick(core, q_raw.at[core])
    row = lax.broadcasted_iota(jnp.int32, (512, 1), 0)
    place = lax.rem(row // 16, 4) * 128 + row // 64 * 16 + lax.rem(row, 16)
    perm[...] = jnp.where(lax.broadcasted_iota(jnp.int32, (512, 512), 1) == place, 1.0, 0.0).astype(BF16)

    def second_copies(half):
        return [
            remote(
                sum1.at[half, wrap(zl + d, 4)], recv2.at[half, d - 1], s2_send.at[half, d - 1],
                s2_recv.at[half, d - 1], device(dzl=d),
            )
            for d in (2, 3, 1)
        ]

    for half in (0, 1):
        for cross in (0, 1):
            plain_copy(half, cross).wait()
            mixed_copy(half, cross).wait()
        twin_copy(half).wait()
        for cross in (0, 1):
            mine = recv1[1, 2, half] if cross else part1[y, core, half]
            total = mine + recv1[cross, 0, half] + recv1[cross, 1, half]
            for q in range(4):
                sum1[half, q, twin if cross else core] = total[:, 256 * q:256 * q + 256]
        for copy in second_copies(half):
            copy.start()

    def third_copies(half):
        low, place = (grad_low, y) if half else (act_low, zl)
        return [
            remote(
                low.at[place], low.at[place], s3_send.at[half, d - 1], s3_recv.at[half, d - 1],
                device(dy=d) if half else device(dzl=d),
            )
            for d in (2, 1, 3)
        ]

    for half in (0, 1):
        for copy in second_copies(half):
            copy.wait()
        total = (sum1[half, zl] + recv2[half, 0] + recv2[half, 1] + recv2[half, 2]).astype(BF16)
        if half:
            grad_low[y] = total
        else:
            act_low[zl] = total
        for copy in third_copies(half):
            copy.start()

    q_copy.wait()

    def reorder(step, carry):
        b, half = step // 2, lax.rem(step, 2)
        columns = pl.ds(pl.multiple_of(step * 512, 512), 512)
        into = pl.ds(pl.multiple_of(half * 128, 128), 128)
        lhs = q_raw[:, :, columns].reshape(2 * QROWS, 512)
        moved = jnp.dot(lhs, perm[...], preferred_element_type=F32).astype(BF16).reshape(2, QROWS, 512)
        for q in range(4):
            q_perm[q * 4 + b, :, :, into] = moved[:, :, 128 * q:128 * q + 128]
        return carry

    lax.fori_loop(0, 8, reorder, 0)
    id_copy.wait()
    for half in (0, 1):
        for copy in third_copies(half):
            copy.wait_send()
    for d in (1, 2, 3):
        remote(
            act_low.at[wrap(zl - d, 4)], act_low.at[wrap(zl - d, 4)],
            s3_send.at[0, d - 1], s3_recv.at[0, d - 1], device(dzl=d),
        ).wait_recv()
        remote(
            grad_low.at[wrap(y - d, 4)], grad_low.at[wrap(y - d, 4)],
            s3_send.at[1, d - 1], s3_recv.at[1, d - 1], device(dy=d),
        ).wait_recv()

    lane = lax.broadcasted_iota(jnp.int32, (16, 256), 1)
    repeat = jnp.where(lane % 16 == lax.broadcasted_iota(jnp.int32, (16, 256), 0), 1.0, 0.0).astype(BF16)

    for row in (0, 1):
        sums = jnp.zeros((256, 16), F32)
        for q in range(4):
            onehot = lax.broadcasted_iota(jnp.int32, (16, 256), 0) == ids2[row, :, 256 * q:256 * q + 256]
            grads = grad_low[q, row].astype(F32)
            for i in range(16):
                spread[16 * i:16 * i + 16, :] = jnp.where(onehot, grads[i:i + 1], 0.0).astype(BF16)
            sums = sums + lax.dot_general(spread[...], act_low[q, row], NT, preferred_element_type=F32)
        wide = jnp.dot(sums.astype(BF16), repeat, preferred_element_type=F32)
        block = jnp.zeros((16, 256), F32)
        for i in range(16):
            block = block + jnp.where(lane // 16 == i, wide[16 * i:16 * i + 16], 0.0)
        blocks[row, 0, 0, 4] = block.astype(BF16)

    reach = (1, 2, 3, 4, -1, -2, -3, -4)
    z1 = {
        d: remote(
            blocks.at[:, 0, 0, 4], blocks.at[:, 0, 0, 4 - d], z1_send.at[k], z1_recv.at[k], along(d)
        )
        for k, d in enumerate(reach)
    }
    for d in (-1, -2, -3, -4, 1, 2, 3, 4):
        z1[d].start()
    beyond = [
        remote(
            blocks.at[:, 0, 0, pl.ds(5, 4)], blocks.at[:, 0, 0, pl.ds(9, 4)], z2_send.at[0], z2_recv.at[0], along(-4)
        ),
        remote(
            blocks.at[:, 0, 0, pl.ds(1, 3)], blocks.at[:, 0, 0, pl.ds(13, 3)], z2_send.at[1], z2_recv.at[1], along(4)
        ),
    ]
    ways = [device(dx=1), device(dx=3), device(dy=1), device(dy=3)]
    groups = (((3, 2), (5, 1)), ((6, 1), (7, 2)), ((0, 2), (2, 1)), ((9, 2), (11, 2)), ((13, 1), (14, 2)))

    def stage(group, n):
        (start, one), (middle, two) = groups[group]
        whole, lower, upper = pl.ds(start, one + two), pl.ds(start, one), pl.ds(middle, two)
        at, both, rest = (lambda *k: blocks.at[k]), slice(None), pl.ds(1, 3)
        if n == 0:
            src = [at(both, 0, 0, whole)] * 4
            dst = [at(both, 0, 3, whole), at(both, 0, 1, whole), at(both, 3, 0, whole), at(both, 1, 0, whole)]
        elif n == 1:
            src = [at(0, 0, 3, whole), at(1, 0, 1, whole), at(0, 3, 0, whole), at(1, 1, 0, whole)]
            dst = [at(0, 0, 2, whole), at(1, 0, 2, whole), at(0, 2, 0, whole), at(1, 2, 0, whole)]
        elif n == 2:
            src = [at(1, rest, 0, whole)] * 2 + [at(0, 0, rest, whole)] * 2
            dst = [at(1, rest, 3, whole), at(1, rest, 1, whole), at(0, 3, rest, whole), at(0, 1, rest, whole)]
        else:
            src = [at(1, rest, 3, lower), at(1, rest, 1, upper), at(0, 3, rest, lower), at(0, 1, rest, upper)]
            dst = [at(1, rest, 2, lower), at(1, rest, 2, upper), at(0, 2, rest, lower), at(0, 2, rest, upper)]
        return [
            remote(src[k], dst[k], xy_send.at[group, n, k], xy_recv.at[group, n, k], ways[k]) for k in range(4)
        ]

    stages = {(group, n): stage(group, n) for group in range(5) for n in range(4)}

    def go(group, n):
        if n:
            before = stages[group, n - 1]
        else:
            before = ([z1[1], z1[-1]], [z1[-2], z1[-3], z1[-4]], [z1[2], z1[3], z1[4]], beyond[:1], beyond[1:])[group]
        for copy in before:
            copy.wait_recv()
        if n < 4:
            for copy in stages[group, n]:
                copy.start()

    def score(group):
        (start, one), (_, two) = groups[group]

        def one_place(place, carry):
            far = lax.rem(z + place + 12, 16)
            zone, b = far // 4, lax.rem(far, 4)
            scores = jnp.zeros((2 * QROWS, 128), F32)
            for dy in range(4):
                lhs = q_perm[wrap(y + dy, 4) * 4 + b].reshape(2 * QROWS, 256)
                rhs = jnp.concatenate(
                    [blocks[half, dy, dx, place] for dx in range(4) for half in (0, 1)], axis=0
                )
                scores = scores + lax.dot_general(lhs, rhs, NT, preferred_element_type=F32)
            part[0, zone] += scores[:QROWS]
            part[1, zone] += scores[QROWS:]
            return carry

        lax.fori_loop(start, start + one + two, one_place, 0)

    part[...] = jnp.zeros_like(part)
    near, far = (0, 1, 2), (3, 4)
    for groups_now, n in [
        (near, 0), (near, 1), (far, 0), (near, 2), (far, 1), (far, 2), (near, 3), (far, 3), (near, 4), (far, 4)
    ]:
        for group in groups_now:
            go(group, n)
            if n == 4:
                score(group)
            if n == 0 and group in (1, 2):
                beyond[group - 1].start()
    swap = remote(part.at[twin], other, o_send.at[0], o_recv.at[0], device(c=twin))
    swap.start()

    for copy in z1.values():
        copy.wait_send()
    for copy in beyond:
        copy.wait_send()
    for copies in stages.values():
        for copy in copies:
            copy.wait_send()
    swap.wait()

    for dx in range(4):
        cols = slice(32 * dx, 32 * dx + 32)
        pieces = [(part[core, zone] + other[zone])[:136, cols] for zone in range(4)]
        out[:, pl.ds(pl.multiple_of(wrap(x + dx, 4) * 128, 128), 128)] = jnp.concatenate(pieces, axis=1)


def local(activations, out_grads, proj_in, proj_out, example_ids, loss_mask, query_grads):
    queries = query_grads.reshape(136, 2, 32, 128).transpose(0, 2, 1, 3).reshape(136 * 64, 128)
    dma = pltpu.SemaphoreType.DMA
    return pl.pallas_call(
        body,
        out_shape=jax.ShapeDtypeStruct((136, 512), F32),
        in_specs=[pl.BlockSpec(memory_space=pl.ANY)] * 7,
        out_specs=pl.BlockSpec(memory_space=pltpu.VMEM),
        scratch_shapes=[
            pltpu.VMEM((2, 1024, 256), BF16),
            pltpu.VMEM((2, 1024, 256), BF16),
            pltpu.VMEM((2, 64, 256), BF16),
            pltpu.VMEM((2, 64, 256), BF16),
            pltpu.VMEM((1, 1024), jnp.int32),
            pltpu.VMEM((1, 1024), jnp.int32),
            pltpu.VMEM((136 * 64, 128), BF16),
            pltpu.VMEM((136 * 64, 128), F32),
            pltpu.VMEM((QROWS, 4096), BF16),
            pltpu.VMEM((4, 2, 2, 16, 1024), F32),
            pltpu.VMEM((2, 2, 16, 1024), F32),
            pltpu.VMEM((2, 2, 16, 1024), F32),
            pltpu.VMEM((2, 3, 2, 16, 1024), F32),
            pltpu.VMEM((2, 4, 2, 16, 256), F32),
            pltpu.VMEM((2, 3, 2, 16, 256), F32),
            pltpu.VMEM((4, 2, 16, 256), BF16),
            pltpu.VMEM((4, 2, 16, 256), BF16),
            pltpu.VMEM((2, 1, 1024), jnp.int32),
            pltpu.VMEM((256, 256), BF16),
            pltpu.VMEM((512, 512), BF16),
            pltpu.VMEM((2, QROWS, 4096), BF16),
            pltpu.VMEM((16, 2, QROWS, 256), BF16),
            pltpu.VMEM((2, 4, 4, 16, 16, 256), BF16),
            pltpu.VMEM((2, 4, QROWS, 128), F32),
            pltpu.VMEM((4, QROWS, 128), F32),
            dma((7,)), dma((2,)), dma((2,)), dma((2,)), dma((2,)), dma((2, 3, 2)), dma((2, 3, 2)),
            dma((2, 3)), dma((2, 3)), dma((2, 3)), dma((2, 3)), dma((8,)), dma((8,)), dma((2,)), dma((2,)),
            dma((5, 4, 4)), dma((5, 4, 4)), dma((1,)), dma((1,)),
        ],
        compiler_params=pltpu.CompilerParams(
            collective_id=0, has_side_effects=True, vmem_limit_bytes=56 * 2**20
        ),
        name="scores",
    )(activations, out_grads, proj_in, proj_out, example_ids, loss_mask, queries)


def solution(mesh):
    in_specs = (
        P(None, "dp", "tensor"),
        P(None, "dp", "tensor"),
        P(None, None, "tensor"),
        P(None, None, "tensor"),
        P("dp", None),
        P("dp", None),
        P(("dp", "tensor"), None, None),
    )
    out_specs = P(("dp", "tensor"), None)
    return jax.shard_map(local, mesh=mesh, in_specs=in_specs, out_specs=out_specs, check_vma=False)
```

time: 83.7 us -> 79.8 us (0.953)
  Pallas kernels: 81.8 us -> 78 us
    pallas_call x1, Pallas kernels: 81.8 us -> 78 us  [local(): pl.pallas_call(body, out_shape=jax.ShapeDtypeStruct((136, 512), F32), in_...]
where the time goes in v3:
time: 79.8 us; the launch traced here: 79.7 us
  Pallas kernels  78 us (98%)
  local copies, waits for them, and re-layouts  1.68 us (2%)
    pallas_call x1, Pallas kernels, local(): pl.pallas_call(body, out_shape=jax.ShapeDtypeStruct((136, 512), F32), in_...  78 us
    unnamed x1, local copies, waits for them, and re-layouts  1.68 us

profile of v3, /device:TPU:1, one launch (start us, length us, event | category | flops | bytes accessed | tf_op | source)
XLA Modules:
  0.0 79.7 jit_solution(5393301413651402022)
XLA Ops:
  0.0 78.0 %scores.1 = f32[136,512]{1,0:T(8,128)} custom-call(bf16[2,1024,256]{2,1,0:T(8,128)(2,1)} %act_hbm.1, bf16[2,1024,256]{2,1,0:T(8,128)(2,1)} %outg_hbm.1, bf16[2,64,256]{2,1,0:T(8,128)(2,1)} %in_hbm.1, bf16[2,64,256]{2,1,0:T(8,128)(2,1)} %out_hbm.1, s32[1,1024]{1,0:T(1,128)} %ids_hbm.1, s32[1,1024]{1,0:T(1,128)} %mask_hbm.1, bf16[8704,128]{1,0:T(8,128)(2,1)} %bitcast.5), custom_call_target="tpu_custom_call" | custom-call | tf_op jit(solution)/shard_map/scores/pallas_call | solution.py:352
  78.0 1.7 %copy.10 = f32[136,512]{1,0:T(8,128)} copy(f32[136,512]{1,0:T(8,128)} %scores.1) | data formatting | bytes 557056

commit v4 on v3

--- a/solution.py
+++ b/solution.py
@@ -16,11 +16,11 @@
 
 
 def body(
-    act_hbm, outg_hbm, in_hbm, out_hbm, ids_hbm, mask_hbm, queries, out,
+    act_hbm, outg_hbm, in_hbm, out_hbm, ids_hbm, mask_hbm, queries, out, got,
     act, outg, proj_in, proj_out, ids, mask, q_pairs, q_wide, q_twin,
-    part1, relay, mixed, recv1, sum1, recv2, act_low, grad_low, ids2, spread, perm, q_raw, q_perm, blocks, part, other,
+    part1, relay, mixed, recv1, sum1, recv2, act_low, grad_low, ids2, spread, perm, q_raw, q_perm, blocks, part, kept, theirs,
     in_sem, q_sem, id_sem, r_send, r_recv, s1_send, s1_recv, s2_send, s2_recv, s3_send, s3_recv, z1_send, z1_recv, z2_send, z2_recv,
-    xy_send, xy_recv, o_send, o_recv,
+    xy_send, xy_recv, o_send, o_recv, keep_sem,
 ):
     dp, tensor = lax.axis_index("dp"), lax.axis_index("tensor")
     x, zh, core = dp // 8, dp // 2 % 4, dp % 2
@@ -38,17 +38,6 @@
         return pltpu.make_async_remote_copy(
             src_ref=src, dst_ref=dst, send_sem=send, recv_sem=recv, device_id=dev, device_id_type=MESH
         )
-
-    def along(d):
-        to = lax.rem(z + 16 + d, 16)
-        return ((x * 4 + to // 4) * 2 + core, lax.rem(to, 4) * 4 + y)
-
-    barrier = pltpu.get_barrier_semaphore()
-    peers = [along(d) for d in (4, -4, 3, -3, 2, -2, 1, -1)]
-    peers += [device(dy=d, c=c) for d in (1, 3) for c in (core, twin)]
-    peers += [device(dy=2), device(dx=1), device(dx=3), device(c=twin)]
-    for peer in peers:
-        pl.semaphore_signal(barrier, inc=1, device_id=peer, device_id_type=MESH)
 
     loads = [
         pltpu.make_async_copy(src, dst, in_sem.at[k])
@@ -59,6 +48,17 @@
     ]
     for load in loads:
         load.start()
+
+    def along(d):
+        to = lax.rem(z + 16 + d, 16)
+        return ((x * 4 + to // 4) * 2 + core, lax.rem(to, 4) * 4 + y)
+
+    barrier = pltpu.get_barrier_semaphore()
+    peers = [along(d) for d in (4, -4, 3, -3, 2, -2, 1, -1)]
+    peers += [device(dy=d, c=c) for d in (1, 3) for c in (core, twin)]
+    peers += [device(dy=2), device(dx=1), device(dx=3), device(c=twin)]
+    for peer in peers:
+        pl.semaphore_signal(barrier, inc=1, device_id=peer, device_id_type=MESH)
 
     loads[0].wait()
     loads[1].wait()
@@ -180,6 +180,20 @@
         for copy in second_copies(half):
             copy.start()
 
+    q_copy.wait()
+
+    def reorder(step, carry):
+        b, half = step // 2, lax.rem(step, 2)
+        columns = pl.ds(pl.multiple_of(step * 512, 512), 512)
+        into = pl.ds(pl.multiple_of(half * 128, 128), 128)
+        lhs = q_raw[:, :, columns].reshape(2 * QROWS, 512)
+        moved = jnp.dot(lhs, perm[...], preferred_element_type=F32).astype(BF16).reshape(2, QROWS, 512)
+        for q in range(4):
+            q_perm[q * 4 + b, :, :, into] = moved[:, :, 128 * q:128 * q + 128]
+        return carry
+
+    lax.fori_loop(0, 4, reorder, 0)
+
     def third_copies(half):
         low, place = (grad_low, y) if half else (act_low, zl)
         return [
@@ -201,19 +215,7 @@
         for copy in third_copies(half):
             copy.start()
 
-    q_copy.wait()
-
-    def reorder(step, carry):
-        b, half = step // 2, lax.rem(step, 2)
-        columns = pl.ds(pl.multiple_of(step * 512, 512), 512)
-        into = pl.ds(pl.multiple_of(half * 128, 128), 128)
-        lhs = q_raw[:, :, columns].reshape(2 * QROWS, 512)
-        moved = jnp.dot(lhs, perm[...], preferred_element_type=F32).astype(BF16).reshape(2, QROWS, 512)
-        for q in range(4):
-            q_perm[q * 4 + b, :, :, into] = moved[:, :, 128 * q:128 * q + 128]
-        return carry
-
-    lax.fori_loop(0, 8, reorder, 0)
+    lax.fori_loop(4, 8, reorder, 0)
     id_copy.wait()
     for half in (0, 1):
         for copy in third_copies(half):
@@ -298,38 +300,55 @@
             for copy in stages[group, n]:
                 copy.start()
 
-    def score(group):
-        (start, one), (_, two) = groups[group]
-
-        def one_place(place, carry):
+    def score(start, pairs, single, who=None):
+        def add(place, places):
             far = lax.rem(z + place + 12, 16)
             zone, b = far // 4, lax.rem(far, 4)
-            scores = jnp.zeros((2 * QROWS, 128), F32)
+            scores = jnp.zeros(((2 if who is None else 1) * QROWS, 128 * len(places)), F32)
             for dy in range(4):
-                lhs = q_perm[wrap(y + dy, 4) * 4 + b].reshape(2 * QROWS, 256)
+                k = wrap(y + dy, 4) * 4 + b
+                lhs = q_perm[k].reshape(2 * QROWS, 256) if who is None else q_perm[k, who]
                 rhs = jnp.concatenate(
-                    [blocks[half, dy, dx, place] for dx in range(4) for half in (0, 1)], axis=0
+                    [blocks[half, dy, dx, place + e] for e in places for dx in range(4) for half in (0, 1)], axis=0
                 )
                 scores = scores + lax.dot_general(lhs, rhs, NT, preferred_element_type=F32)
-            part[0, zone] += scores[:QROWS]
-            part[1, zone] += scores[QROWS:]
+            for k in range(len(places)):
+                for n, rows in enumerate((0, 1) if who is None else (who,)):
+                    part[rows, lax.rem(zone + k, 4)] += scores[QROWS * n:QROWS * n + QROWS, 128 * k:128 * k + 128]
+
+        def add_pair(place, carry):
+            add(place, (0, 4))
             return carry
 
-        lax.fori_loop(start, start + one + two, one_place, 0)
+        lax.fori_loop(start, start + pairs, add_pair, 0)
+        add(single, (0,))
 
     part[...] = jnp.zeros_like(part)
     near, far = (0, 1, 2), (3, 4)
     for groups_now, n in [
-        (near, 0), (near, 1), (far, 0), (near, 2), (far, 1), (far, 2), (near, 3), (far, 3), (near, 4), (far, 4)
+        (near, 0), (near, 1), (far, 0), (far, 1), (near, 2), (far, 2), (near, 3), (far, 3), (near, 4), (far, 4)
     ]:
         for group in groups_now:
             go(group, n)
-            if n == 4:
-                score(group)
             if n == 0 and group in (1, 2):
                 beyond[group - 1].start()
-    swap = remote(part.at[twin], other, o_send.at[0], o_recv.at[0], device(c=twin))
+        if n == 4 and groups_now == near:
+            score(0, 4, 8)
+
+    def arrange(rows, into):
+        for dx in range(4):
+            cols = slice(32 * dx, 32 * dx + 32)
+            pieces = [part[rows, zone][:136, cols] for zone in range(4)]
+            into[:, pl.ds(pl.multiple_of(wrap(x + dx, 4) * 128, 128), 128)] = jnp.concatenate(pieces, axis=1)
+
+    score(9, 3, 12, twin)
+    arrange(twin, theirs)
+    swap = remote(theirs, got, o_send.at[0], o_recv.at[0], device(c=twin))
     swap.start()
+    score(9, 3, 12, core)
+    arrange(core, kept)
+    keep = pltpu.make_async_copy(kept, out, keep_sem)
+    keep.start()
 
     for copy in z1.values():
         copy.wait_send()
@@ -338,22 +357,18 @@
     for copies in stages.values():
         for copy in copies:
             copy.wait_send()
+    keep.wait()
     swap.wait()
-
-    for dx in range(4):
-        cols = slice(32 * dx, 32 * dx + 32)
-        pieces = [(part[core, zone] + other[zone])[:136, cols] for zone in range(4)]
-        out[:, pl.ds(pl.multiple_of(wrap(x + dx, 4) * 128, 128), 128)] = jnp.concatenate(pieces, axis=1)
 
 
 def local(activations, out_grads, proj_in, proj_out, example_ids, loss_mask, query_grads):
     queries = query_grads.reshape(136, 2, 32, 128).transpose(0, 2, 1, 3).reshape(136 * 64, 128)
     dma = pltpu.SemaphoreType.DMA
-    return pl.pallas_call(
+    own, received = pl.pallas_call(
         body,
-        out_shape=jax.ShapeDtypeStruct((136, 512), F32),
+        out_shape=[jax.ShapeDtypeStruct((136, 512), F32)] * 2,
         in_specs=[pl.BlockSpec(memory_space=pl.ANY)] * 7,
-        out_specs=pl.BlockSpec(memory_space=pltpu.VMEM),
+        out_specs=[pl.BlockSpec(memory_space=pl.ANY)] * 2,
         scratch_shapes=[
             pltpu.VMEM((2, 1024, 256), BF16),
             pltpu.VMEM((2, 1024, 256), BF16),
@@ -379,16 +394,18 @@
             pltpu.VMEM((16, 2, QROWS, 256), BF16),
             pltpu.VMEM((2, 4, 4, 16, 16, 256), BF16),
             pltpu.VMEM((2, 4, QROWS, 128), F32),
-            pltpu.VMEM((4, QROWS, 128), F32),
+            pltpu.VMEM((136, 512), F32),
+            pltpu.VMEM((136, 512), F32),
             dma((7,)), dma((2,)), dma((2,)), dma((2,)), dma((2,)), dma((2, 3, 2)), dma((2, 3, 2)),
             dma((2, 3)), dma((2, 3)), dma((2, 3)), dma((2, 3)), dma((8,)), dma((8,)), dma((2,)), dma((2,)),
-            dma((5, 4, 4)), dma((5, 4, 4)), dma((1,)), dma((1,)),
+            dma((5, 4, 4)), dma((5, 4, 4)), dma((1,)), dma((1,)), dma,
         ],
         compiler_params=pltpu.CompilerParams(
             collective_id=0, has_side_effects=True, vmem_limit_bytes=56 * 2**20
         ),
         name="scores",
     )(activations, out_grads, proj_in, proj_out, example_ids, loss_mask, queries)
+    return own + received
 
 
 def solution(mesh):

time: 79.8 us -> 77.4 us (0.970)
  Pallas kernels: 78 us -> 75.5 us
  other arithmetic: 0 us -> 1.79 us
  local copies, waits for them, and re-layouts: 1.68 us -> 0 us
    pallas_call x1, Pallas kernels: 78 us -> 75.5 us  [local(): pl.pallas_call(body, out_shape=[jax.ShapeDtypeStruct((136, 512), F32)] *...]
    add x0 -> x1, other arithmetic: none -> 1.79 us  [local(): return own + received]
    unnamed x1 -> x0, local copies, waits for them, and re-layouts: 1.68 us -> none
where the time goes in v4:
time: 77.4 us; the launch traced here: 77.3 us
  Pallas kernels  75.5 us (98%)
  other arithmetic  1.79 us (2%)
    pallas_call x1, Pallas kernels, local(): pl.pallas_call(body, out_shape=[jax.ShapeDtypeStruct((136, 512), F32)] *...  75.5 us
    add x1, other arithmetic, local(): return own + received  1.79 us

profile of v4, /device:TPU:1, one launch (start us, length us, event | category | flops | bytes accessed | tf_op | source)
XLA Modules:
  0.0 77.3 jit_solution(4593400045764972345)
XLA Ops:
  0.0 75.5 %scores.1 = (f32[136,512]{1,0:T(8,128)}, f32[136,512]{1,0:T(8,128)}) custom-call(bf16[2,1024,256]{2,1,0:T(8,128)(2,1)} %act_hbm.1, bf16[2,1024,256]{2,1,0:T(8,128)(2,1)} %outg_hbm.1, bf16[2,64,256]{2,1,0:T(8,128)(2,1)} %in_hbm.1, bf16[2,64,256]{2,1,0:T(8,128)(2,1)} %out_hbm.1, s32[1,1024]{1,0:T(1,128)} %ids_hbm.1, s32[1,1024]{1,0:T(1,128)} %mask_hbm.1, ...), custom_call_target="tpu_custom_call" | custom-call | tf_op jit(solution)/shard_map/scores/pallas_call | solution.py:367
  75.5 1.8 %add.3 = f32[136,512]{1,0:T(8,128)} add(f32[136,512]{1,0:T(8,128)} %get-tuple-element.7, f32[136,512]{1,0:T(8,128)} %get-tuple-element.8) | non-fusion elementwise | flops 69632 | bytes 835584 | tf_op jit(solution)/shard_map/add | solution.py:408

commit v5 on v4

--- a/solution.py
+++ b/solution.py
@@ -19,7 +19,7 @@
     act_hbm, outg_hbm, in_hbm, out_hbm, ids_hbm, mask_hbm, queries, out, got,
     act, outg, proj_in, proj_out, ids, mask, q_pairs, q_wide, q_twin,
     part1, relay, mixed, recv1, sum1, recv2, act_low, grad_low, ids2, spread, perm, q_raw, q_perm, blocks, part, kept, theirs,
-    in_sem, q_sem, id_sem, r_send, r_recv, s1_send, s1_recv, s2_send, s2_recv, s3_send, s3_recv, z1_send, z1_recv, z2_send, z2_recv,
+    vouch, in_sem, q_sem, id_sem, r_send, r_recv, s1_send, s1_recv, s2_send, s2_recv, s3_send, s3_recv, z1_send, z1_recv, z2_send, z2_recv,
     xy_send, xy_recv, o_send, o_recv, keep_sem,
 ):
     dp, tensor = lax.axis_index("dp"), lax.axis_index("tensor")
@@ -54,28 +54,28 @@
         return ((x * 4 + to // 4) * 2 + core, lax.rem(to, 4) * 4 + y)
 
     barrier = pltpu.get_barrier_semaphore()
-    peers = [along(d) for d in (4, -4, 3, -3, 2, -2, 1, -1)]
+    peers = [along(1), along(-1), device(dx=1), device(dx=3), device(c=twin)]
     peers += [device(dy=d, c=c) for d in (1, 3) for c in (core, twin)]
-    peers += [device(dy=2), device(dx=1), device(dx=3), device(c=twin)]
+
+    def vouch_for(n):
+        pl.semaphore_signal(vouch.at[n, 0], inc=1, device_id=along(1), device_id_type=MESH)
+        pl.semaphore_signal(vouch.at[n, 1], inc=1, device_id=along(-1), device_id_type=MESH)
+
+    def hear(n):
+        pl.semaphore_wait(vouch.at[n, 0], 1)
+        pl.semaphore_wait(vouch.at[n, 1], 1)
+
     for peer in peers:
         pl.semaphore_signal(barrier, inc=1, device_id=peer, device_id_type=MESH)
 
     loads[0].wait()
     loads[1].wait()
 
-    def project_act(layer, carry):
-        a = lax.dot_general(proj_in[layer], act[layer], NT, preferred_element_type=F32)
-        for q in range(4):
-            part1[q, layer, 0] = a[16 * q:16 * q + 16]
-        return carry
-
-    lax.fori_loop(0, 2, project_act, 0)
-    pl.semaphore_wait(barrier, len(peers))
-
-    def relay_copy(half):
+    def relay_copy(half, layer):
         d = 3 if half else 1
         return remote(
-            part1.at[wrap(y + 2, 4), :, half], relay.at[half], r_send.at[half], r_recv.at[half], device(dy=d)
+            part1.at[wrap(y + 2, 4), layer, half], relay.at[half, layer], r_send.at[half, layer],
+            r_recv.at[half, layer], device(dy=d),
         )
 
     def plain_copy(half, cross):
@@ -88,7 +88,7 @@
 
     def mixed_copy(half, cross):
         d = 3 if half else 1
-        c = twin if cross else core
+        c = lax.rem(core + cross, 2)
         return remote(
             mixed.at[half, c], recv1.at[cross, 1, half], s1_send.at[cross, 1, half],
             s1_recv.at[cross, 1, half], device(dy=d, c=c),
@@ -100,23 +100,25 @@
             device(c=twin),
         )
 
-    relay_copy(0).start()
+    for layer in (0, 1):
+        a = lax.dot_general(proj_in[layer], act[layer], NT, preferred_element_type=F32)
+        for q in range(4):
+            part1[q, layer, 0] = a[16 * q:16 * q + 16]
+        if layer == 0:
+            pl.semaphore_wait(barrier, len(peers))
+            vouch_for(0)
+        relay_copy(0, layer).start()
     for cross in (0, 1):
         plain_copy(0, cross).start()
     twin_copy(0).start()
     for load in loads[2:5]:
         load.wait()
-
-    def project_grad(layer, carry):
+    for layer in (0, 1):
         g = lax.dot_general(proj_out[layer], outg[layer], NT, preferred_element_type=F32) * mask[...].astype(F32)
         for q in range(4):
             for i in range(4):
                 part1[q, layer, 1, :, 256 * i:256 * i + 256] = g[16 * i:16 * i + 16, 256 * q:256 * q + 256]
-        return carry
-
-    lax.fori_loop(0, 2, project_grad, 0)
-
-    relay_copy(1).start()
+        relay_copy(1, layer).start()
     for cross in (0, 1):
         plain_copy(1, cross).start()
     twin_copy(1).start()
@@ -125,6 +127,9 @@
     id_copy = remote(ids, ids2.at[core], id_sem.at[0], id_sem.at[1], device(c=twin))
     id_copy.start()
 
+    hear(0)
+    vouch_for(1)
+
     loads[6].wait()
 
     def widen(step, carry):
@@ -148,10 +153,13 @@
     q_copy.start()
 
     for half in (0, 1):
-        relay_copy(half).wait()
-        mixed[half] = relay[half] + part1[wrap(y + (3 if half else 1), 4), :, half]
-        for cross in (0, 1):
-            mixed_copy(half, cross).start()
+        for layer in (0, 1):
+            relay_copy(half, layer).wait()
+            mixed[half, layer] = relay[half, layer] + part1[wrap(y + (3 if half else 1), 4), layer, half]
+            mixed_copy(half, jnp.where(core == layer, 0, 1)).start()
+
+    hear(1)
+    vouch_for(2)
 
     pick(core, q_raw.at[core])
     row = lax.broadcasted_iota(jnp.int32, (512, 1), 0)
@@ -254,6 +262,7 @@
         )
         for k, d in enumerate(reach)
     }
+    hear(2)
     for d in (-1, -2, -3, -4, 1, 2, 3, 4):
         z1[d].start()
     beyond = [
@@ -396,7 +405,7 @@
             pltpu.VMEM((2, 4, QROWS, 128), F32),
             pltpu.VMEM((136, 512), F32),
             pltpu.VMEM((136, 512), F32),
-            dma((7,)), dma((2,)), dma((2,)), dma((2,)), dma((2,)), dma((2, 3, 2)), dma((2, 3, 2)),
+            pltpu.SemaphoreType.REGULAR((3, 2)), dma((7,)), dma((2,)), dma((2,)), dma((2, 2)), dma((2, 2)), dma((2, 3, 2)), dma((2, 3, 2)),
             dma((2, 3)), dma((2, 3)), dma((2, 3)), dma((2, 3)), dma((8,)), dma((8,)), dma((2,)), dma((2,)),
             dma((5, 4, 4)), dma((5, 4, 4)), dma((1,)), dma((1,)), dma,
         ],

time: 77.4 us -> 76 us (0.982)
  Pallas kernels: 75.5 us -> 74.1 us
    pallas_call x1, Pallas kernels: 75.5 us -> 74.1 us  [local(): pl.pallas_call(body, out_shape=[jax.ShapeDtypeStruct((136, 512), F32)] *...]
where the time goes in v5:
time: 76 us; the launch traced here: 75.9 us
  Pallas kernels  74.1 us (97%)
  other arithmetic  1.79 us (2%)
    pallas_call x1, Pallas kernels, local(): pl.pallas_call(body, out_shape=[jax.ShapeDtypeStruct((136, 512), F32)] *...  74.1 us
    add x1, other arithmetic, local(): return own + received  1.79 us

profile of v5, /device:TPU:1, one launch (start us, length us, event | category | flops | bytes accessed | tf_op | source)
XLA Modules:
  0.0 75.9 jit_solution(16885615657434851936)
XLA Ops:
  0.0 74.1 %scores.1 = (f32[136,512]{1,0:T(8,128)}, f32[136,512]{1,0:T(8,128)}) custom-call(bf16[2,1024,256]{2,1,0:T(8,128)(2,1)} %act_hbm.1, bf16[2,1024,256]{2,1,0:T(8,128)(2,1)} %outg_hbm.1, bf16[2,64,256]{2,1,0:T(8,128)(2,1)} %in_hbm.1, bf16[2,64,256]{2,1,0:T(8,128)(2,1)} %out_hbm.1, s32[1,1024]{1,0:T(1,128)} %ids_hbm.1, s32[1,1024]{1,0:T(1,128)} %mask_hbm.1, ...), custom_call_target="tpu_custom_call" | custom-call | tf_op jit(solution)/shard_map/scores/pallas_call | solution.py:376
  74.1 1.8 %add.3 = f32[136,512]{1,0:T(8,128)} add(f32[136,512]{1,0:T(8,128)} %get-tuple-element.7, f32[136,512]{1,0:T(8,128)} %get-tuple-element.8) | non-fusion elementwise | flops 69632 | bytes 835584 | tf_op jit(solution)/shard_map/add | solution.py:417

commit v6 on v5

--- a/solution.py
+++ b/solution.py
@@ -386,7 +386,7 @@
             pltpu.VMEM((1, 1024), jnp.int32),
             pltpu.VMEM((1, 1024), jnp.int32),
             pltpu.VMEM((136 * 64, 128), BF16),
-            pltpu.VMEM((136 * 64, 128), F32),
+            pltpu.VMEM((137 * 64, 128), F32),
             pltpu.VMEM((QROWS, 4096), BF16),
             pltpu.VMEM((4, 2, 2, 16, 1024), F32),
             pltpu.VMEM((2, 2, 16, 1024), F32),

time: 76 us -> 76 us (level)
  no operation moved by 1% of the time
where the time goes in v6:
time: 76 us; the launch traced here: 75.9 us
  Pallas kernels  74.1 us (97%)
  other arithmetic  1.79 us (2%)
    pallas_call x1, Pallas kernels, local(): pl.pallas_call(body, out_shape=[jax.ShapeDtypeStruct((136, 512), F32)] *...  74.1 us
    add x1, other arithmetic, local(): return own + received  1.79 us

profile of v6, /device:TPU:1, one launch (start us, length us, event | category | flops | bytes accessed | tf_op | source)
XLA Modules:
  0.0 75.9 jit_solution(6451958664859596147)
XLA Ops:
  0.0 74.1 %scores.1 = (f32[136,512]{1,0:T(8,128)}, f32[136,512]{1,0:T(8,128)}) custom-call(bf16[2,1024,256]{2,1,0:T(8,128)(2,1)} %act_hbm.1, bf16[2,1024,256]{2,1,0:T(8,128)(2,1)} %outg_hbm.1, bf16[2,64,256]{2,1,0:T(8,128)(2,1)} %in_hbm.1, bf16[2,64,256]{2,1,0:T(8,128)(2,1)} %out_hbm.1, s32[1,1024]{1,0:T(1,128)} %ids_hbm.1, s32[1,1024]{1,0:T(1,128)} %mask_hbm.1, ...), custom_call_target="tpu_custom_call" | custom-call | tf_op jit(solution)/shard_map/scores/pallas_call | solution.py:376
  74.1 1.8 %add.3 = f32[136,512]{1,0:T(8,128)} add(f32[136,512]{1,0:T(8,128)} %get-tuple-element.7, f32[136,512]{1,0:T(8,128)} %get-tuple-element.8) | non-fusion elementwise | flops 69632 | bytes 835584 | tf_op jit(solution)/shard_map/add | solution.py:417
